TPU v7x, 32 devices: a whole 2x2x4 slice. The times are simulated.
32 devices in a mesh: groups: 2 (over y), dp: 4 (over z), owner: 2 (over x), sub: 2 (over core).
Axes of the slice: x: 2, y: 2, z: 4, core: 2. Of those that a mesh axis runs over, the one named last changes fastest.
Arguments:
- ex_acts: bfloat16 [48, 16, 5120], P(('groups', 'dp'), None, ('owner', 'sub')), parts along dimension 0, may hold values from -6 to 6
- ex_grads: bfloat16 [48, 16, 8, 1280], P(('groups', 'dp'), None, 'owner', 'sub'), parts along dimension 0, may hold values from -0.008972168 to 0.008972168
- ex_mask: int32 [48, 16], P(('groups', 'dp')), parts along dimension 0, may hold values 0 or 1
- ex_ids: int32 [48], P(('groups', 'dp')), parts along dimension 0, may hold values from 0 to 23, each once
- query_acts: bfloat16 [32, 16, 5120], P('groups', None, ('owner', 'sub')), parts along dimension 0, may hold values from -6 to 6
- query_grads: bfloat16 [32, 16, 8, 1280], P('groups', None, 'owner', 'sub'), parts along dimension 0, may hold values from -0.008972168 to 0.008972168
- input_basis: bfloat16 [5120, 5120], P(('owner', 'sub'), 'dp'), may hold values from -0.078125 to 0.078125
- hidden_basis: bfloat16 [8, 1280, 1280], P('owner', 'dp', 'sub'), may hold values from -0.15625 to 0.15625
- eigenvalues: float32 [5120, 8, 1280], P('dp', 'owner', 'sub'), may hold values from 0.05 to 5
Outputs:
- scores: float32 [32, 24], P('groups', 'dp'), parts along dimension 0
There are 2 independent parts, one for each index of `groups`. A program takes and returns all parts, laid end to end along the dimension named above; an argument that names none is the same for every part. Nothing has to cross between parts.
Inputs may be any that keep to these rules, and one draw needn't show every extreme that they name: `ex_mask`: 1 keeps a token position, 0 drops it. A permutation: the example at position n is scored in column ex_ids[n].
All inputs are finite; a program needn't handle non-finite values. No bound on the sum of `ex_mask` on one device may be relied on, other than what follows from the above.
Results may differ from a plain program's by a relative error of at most 0.0052.
Values may be sent and summed in bfloat16 or wider, within the bound.
No kernel may reach another device: no remote copies, remote signals or barrier semaphores. Data moves between devices by JAX's collectives and lax.ppermute only.
A program may use at most 448 MiB of HBM per device.

v0:
```python
import functools

import jax
import jax.numpy as jnp
from jax import lax
from jax.experimental import pallas as pl
from jax.experimental.pallas import tpu as pltpu
from jax.sharding import PartitionSpec as P

DAMP = 0.05
BF = jnp.bfloat16
F32 = jnp.float32
MIB = 1024 * 1024
ANY = pl.BlockSpec(memory_space=pl.ANY)
VMEM = pl.BlockSpec(memory_space=pltpu.VMEM)
SMEM = pl.BlockSpec(memory_space=pltpu.SMEM)


def dot(a, b):
    return jnp.dot(a, b, preferred_element_type=F32)


def swap(x, axis):
    return lax.ppermute(x, axis, [(0, 1), (1, 0)])


def ring(x, n):
    parts = [x]
    for _ in range(n - 1):
        parts.append(lax.ppermute(parts[-1], "dp", [(i, (i + 1) % n) for i in range(n)]))
    return parts


def weight_kernel(blocks, step, lam, w, buf, sems):
    i, count = pl.program_id(0), pl.num_programs(0)
    per = count // blocks

    def copy(j, slot):
        def go(b):
            return pltpu.make_async_copy(
                lam.at[pl.ds(pl.multiple_of(lax.rem(j, per) * step, 8), step), b, :],
                buf.at[slot],
                sems.at[slot],
            )
        return go

    def start(j, slot):
        for b in range(blocks):
            pl.when(j // per == b)(lambda b=b: copy(j, slot)(b).start())

    @pl.when(i == 0)
    def _():
        start(i, 0)

    @pl.when(i + 1 < count)
    def _():
        start(i + 1, lax.rem(i + 1, 2))

    slot = lax.rem(i, 2)
    copy(i, slot)(0).wait()
    w[...] = 1.0 / (buf[slot] + DAMP)


def weights(lam):
    j_rows, blocks, width = lam.shape
    step = 320 if j_rows % 320 == 0 else j_rows
    return pl.pallas_call(
        functools.partial(weight_kernel, blocks, step),
        grid=(blocks * (j_rows // step),),
        out_shape=jax.ShapeDtypeStruct((blocks * j_rows, width), F32),
        in_specs=[ANY],
        out_specs=pl.BlockSpec((step, width), lambda i: (i, 0)),
        scratch_shapes=[pltpu.VMEM((2, step, width), F32), pltpu.SemaphoreType.DMA((2,))],
        compiler_params=pltpu.CompilerParams(vmem_limit_bytes=24 * MIB),
        cost_estimate=pl.CostEstimate(
            flops=4 * lam.size, bytes_accessed=8 * lam.size, transcendentals=0
        ),
        name="weights",
    )(lam)


def score_kernel(n, q_count, seq, first, idx, ei, qit, w, basis, q_own, q_oth, *rest):
    xs, zs, rest = rest[:n], rest[n : 2 * n], rest[2 * n :]
    out, full, tok_own, tok_oth, hid, wv, p0, p1, acc, sems, w_sem = rest
    sub = idx[0]
    chunk, all_rows, width = full.shape
    half_rows = all_rows // 2
    q_rows, e_rows = q_own.shape[1], xs[0].shape[1]
    j_rows = ei.shape[1]
    ex_count = ei.shape[0] // seq
    per = 128 // seq
    columns = chunk * width

    moves, w_moves = [], []
    for j in range(chunk):
        b = first + j
        moves.append((basis.at[j], full.at[j]))
        for own, oth, at, size in [(q_own, q_oth, 0, q_rows)] + [
            (xs[k], zs[k], q_rows + k * e_rows, e_rows) for k in range(n)
        ]:
            moves.append((own.at[b], tok_own.at[j, pl.ds(at, size), :]))
            moves.append((oth.at[b], tok_oth.at[j, pl.ds(at, size), :]))
        w_moves.append((w.at[pl.ds(b * j_rows, j_rows), :], wv.at[:, pl.ds(j * width, width)]))
    copies = [pltpu.make_async_copy(a, c, sems.at[i]) for i, (a, c) in enumerate(moves)]
    w_copies = [pltpu.make_async_copy(a, c, w_sem.at[i]) for i, (a, c) in enumerate(w_moves)]
    for copy in copies + w_copies:
        copy.start()
    acc[...] = jnp.zeros_like(acc)
    for copy in copies:
        copy.wait()
    for j in range(chunk):
        b_own = full[j, pl.ds(pl.multiple_of(sub * half_rows, 16), half_rows), :]
        b_oth = full[j, pl.ds(pl.multiple_of((1 - sub) * half_rows, 16), half_rows), :]
        rotated = dot(tok_own[j], b_own) + dot(tok_oth[j], b_oth)
        hid[:, j * width : (j + 1) * width] = rotated.astype(BF)
    for copy in w_copies:
        copy.wait()

    m_step = j_rows // 2
    tiles = [(at, min(256, columns - at)) for at in range(0, columns, 256)]

    def outer(q, dst, at, size):
        grp_q = q // per
        rhs = hid[pl.ds(pl.multiple_of(grp_q * 128, 128), 128), at : at + size]
        row = lax.broadcasted_iota(jnp.int32, rhs.shape, 0) // seq
        rhs = jnp.where(row == q - grp_q * per, rhs.astype(F32), 0.0).astype(BF)
        for m in range(0, j_rows, m_step):
            grad = dot(qit[grp_q, m : m + m_step, :], rhs)
            dst[m : m + m_step, at : at + size] = (
                grad * wv[m : m + m_step, at : at + size]
            ).astype(BF)

    def score(src, at, size):
        prod = dot(ei[...], src[:, at : at + size]) * hid[q_rows:, at : at + size].astype(F32)
        part = sum(prod[:, i : i + 128] for i in range(0, size, 128))
        return part.reshape(ex_count, seq // 8, 8, 128).sum(1)

    def step(q, src, dst):
        part = 0.0
        for at, size in tiles:
            if src is not None:
                part = part + score(src, at, size)
            if dst is not None:
                outer(q + 1, dst, at, size)
        if src is not None:
            acc[q] = part

    step(-1, None, p0)

    def pair(i, carry):
        step(2 * i, p0, p1)
        step(2 * i + 1, p1, p0)
        return carry

    lax.fori_loop(0, q_count // 2 - 1, pair, 0)
    step(q_count - 2, p0, p1)
    step(q_count - 1, p1, None)
    out[...] = acc[...].sum(2)


def chunk_scores(n, q_count, seq, first, idx, ei, qit, w, basis, q_own, q_oth, xs, zs):
    chunk, all_rows, width = basis.shape
    ex_rows, j_rows = ei.shape
    q_rows = q_own.shape[1]
    ex_count = ex_rows // seq
    tokens = pltpu.VMEM((chunk, q_rows + ex_rows, width), BF)
    flops = 2 * q_count * j_rows * chunk * width * (256 + ex_rows)
    return pl.pallas_call(
        functools.partial(score_kernel, n, q_count, seq, first),
        out_shape=jax.ShapeDtypeStruct((q_count, ex_count, 128), F32),
        in_specs=[SMEM, VMEM, VMEM] + [ANY] * (4 + 2 * n),
        out_specs=VMEM,
        scratch_shapes=[
            pltpu.VMEM((chunk, all_rows, width), BF),
            tokens,
            tokens,
            pltpu.VMEM((q_rows + ex_rows, chunk * width), BF),
            pltpu.VMEM((j_rows, chunk * width), F32),
            pltpu.VMEM((j_rows, chunk * width), BF),
            pltpu.VMEM((j_rows, chunk * width), BF),
            pltpu.VMEM((q_count, ex_count, 8, 128), F32),
            pltpu.SemaphoreType.DMA((chunk * (3 + 2 * n),)),
            pltpu.SemaphoreType.DMA((chunk,)),
        ],
        compiler_params=pltpu.CompilerParams(vmem_limit_bytes=52 * MIB),
        cost_estimate=pl.CostEstimate(flops=flops, bytes_accessed=12 * MIB, transcendentals=0),
        name="chunk_scores",
    )(idx, ei, qit, w, basis, q_own, q_oth, *xs, *zs)


def sum_features(part, sub, sizes):
    half = part.shape[0] // 2
    mine = lax.dynamic_slice_in_dim(part, sub * half, half, 0)
    other = lax.dynamic_slice_in_dim(part, (1 - sub) * half, half, 0).astype(BF)
    mine = mine + swap(other, "sub").astype(F32)
    if sizes["owner"] == 2:
        total = mine + swap(mine.astype(BF), "owner").astype(F32)
    else:
        total = lax.psum(mine, "owner")
    total = total.astype(BF)
    rest = swap(total, "sub")
    return jnp.where(
        sub == 0, jnp.concatenate([total, rest], 0), jnp.concatenate([rest, total], 0)
    )


def shards(
    sizes,
    ex_acts,
    ex_grads,
    ex_mask,
    ex_ids,
    query_acts,
    query_grads,
    input_basis,
    hidden_basis,
    eigenvalues,
):
    n = sizes["dp"]
    dpi, grp, sub = (lax.axis_index(a) for a in ("dp", "groups", "sub"))
    ex_count, seq, input_cols = ex_acts.shape
    q_count, q_seq, _ = query_acts.shape
    blocks, rows, width = hidden_basis.shape
    j_rows = input_basis.shape[1]
    e_rows, q_rows = ex_count * seq, q_count * q_seq
    share = sizes["groups"] == 2 and rows % 32 == 0
    idx = sub.astype(jnp.int32).reshape(1)

    acts = ring(ex_acts.reshape(e_rows, input_cols), n)
    keep = ex_mask.astype(BF).reshape(e_rows, 1, 1)
    e_raw = jnp.transpose(ex_grads.reshape(e_rows, blocks, width) * keep, (1, 0, 2))
    q_raw = jnp.transpose(query_grads.reshape(q_rows, blocks, width), (1, 0, 2))
    xs = ring(e_raw, n)
    zs = [swap(x, "sub") for x in xs]
    q_oth = swap(q_raw, "sub")
    all_ids = jnp.concatenate(ring(ex_ids, n))

    chunk = 2 if blocks % 2 == 0 else 1
    mine = hidden_basis
    if share:
        mine = lax.dynamic_slice_in_dim(hidden_basis, grp * (rows // 2), rows // 2, 1)
    full = [
        lax.all_gather(
            mine[b : b + chunk], ("dp", "groups") if share else "dp", axis=1, tiled=True
        )
        for b in range(0, blocks, chunk)
    ]

    q_in = sum_features(dot(query_acts.reshape(q_rows, input_cols), input_basis), sub, sizes)
    qit = jnp.transpose(q_in.reshape(q_rows // 128, 128, j_rows), (0, 2, 1))
    w = weights(eigenvalues)
    ei = sum_features(dot(jnp.concatenate(acts, 0), input_basis), sub, sizes)

    total = 0.0
    for i, basis in enumerate(full):
        total = total + chunk_scores(
            n, q_count, seq, i * chunk, idx, ei, qit, w, basis, q_raw, q_oth, xs, zs
        )
    scores = total.sum(2)

    ex_total = all_ids.shape[0]
    onehot = (all_ids[:, None] == jnp.arange(ex_total, dtype=jnp.int32)[None, :]).astype(F32)
    placed = jnp.dot(scores, onehot, precision=lax.Precision.HIGHEST, preferred_element_type=F32)
    if sizes["owner"] == 2:
        pairs = [[(i, i ^ k) for i in range(4)] for k in (1, 2, 3)]
        placed = placed + sum(lax.ppermute(placed, ("owner", "sub"), p) for p in pairs)
    else:
        placed = lax.psum(placed, ("owner", "sub"))

    def columns(device):
        return lax.dynamic_slice_in_dim(placed, lax.rem(device, n) * ex_count, ex_count, 1)

    result = columns(dpi)
    for k in range(1, n):
        pairs = [(i, (i + k) % n) for i in range(n)]
        result = result + lax.ppermute(columns(dpi + k), "dp", pairs)
    return result


def solution(mesh):
    in_specs = (
        P(("groups", "dp"), None, ("owner", "sub")),
        P(("groups", "dp"), None, "owner", "sub"),
        P(("groups", "dp"), None),
        P(("groups", "dp")),
        P("groups", None, ("owner", "sub")),
        P("groups", None, "owner", "sub"),
        P(("owner", "sub"), "dp"),
        P("owner", "dp", "sub"),
        P("dp", "owner", "sub"),
    )
    out_specs = P("groups", "dp")
    body = functools.partial(shards, dict(mesh.shape))
    return jax.shard_map(body, mesh=mesh, in_specs=in_specs, out_specs=out_specs, check_vma=False)
```

profile of v0, /device:TPU:0, one launch (start us, length us, event | category | flops | bytes accessed | tf_op | source)
XLA Modules:
  0.0 246.1 jit_solution(13066130553912164845)
XLA Ops:
  6.6 2.3 constant_dynamic-slice_fusion.4
  8.9 3.1 %collective-permute-start = (bf16[96,1280]{1,0:T(8,128)(2,1)S(1)}, bf16[96,1280]{1,0:T(8,128)(2,1)}, u32[]{:S(2)}, u32[]{:S(2)}) collective-permute-start(bf16[96,1280]{1,0:T(8,128)(2,1)S(1)} %bitcast.19), channel_id=1, source_target_pairs={{0,4},{4,8},{8,12},{12,0},{1,5},{5,9},{9,13},{13,1},{2,6},{6,10},{... | collective-permute-start | bytes 737288 | tf_op jit(solution)/shard_map/ppermute | solution.py:30
  12.0 8.1 %collective-permute-done = bf16[96,1280]{1,0:T(8,128)(2,1)} collective-permute-done((bf16[96,1280]{1,0:T(8,128)(2,1)S(1)}, bf16[96,1280]{1,0:T(8,128)(2,1)}, u32[]{:S(2)}, u32[]{:S(2)}) %collective-permute-start) | collective-permute-done | bytes 245792 | tf_op jit(solution)/shard_map/ppermute | solution.py:30
  22.1 12.7 %collective-permute-done.1 = bf16[96,1280]{1,0:T(8,128)(2,1)} collective-permute-done((bf16[96,1280]{1,0:T(8,128)(2,1)}, bf16[96,1280]{1,0:T(8,128)(2,1)}, u32[]{:S(2)}, u32[]{:S(2)}) %collective-permute-start.1) | collective-permute-done | bytes 245792 | tf_op jit(solution)/shard_map/ppermute | solution.py:30
  36.7 3.6 %collective-permute-start.10 = (bf16[4,96,640]{2,1,0:T(8,128)(2,1)}, bf16[4,96,640]{2,1,0:T(8,128)(2,1)}, u32[]{:S(2)}, u32[]{:S(2)}) collective-permute-start(bf16[4,96,640]{2,1,0:T(8,128)(2,1)} %bitcast.9.rest_0_), channel_id=1, source_target_pairs={{0,4},{4,8},{8,12},{12,0},{1,5},{5,9},{9,13},{13,1},{2,6},{6,10},{... | collective-permute-start | bytes 1474568 | tf_op jit(solution)/shard_map/ppermute | solution.py:30
  40.3 9.8 %collective-permute-done.2 = bf16[96,1280]{1,0:T(8,128)(2,1)} collective-permute-done((bf16[96,1280]{1,0:T(8,128)(2,1)}, bf16[96,1280]{1,0:T(8,128)(2,1)}, u32[]{:S(2)}, u32[]{:S(2)}) %collective-permute-start.2) | collective-permute-done | bytes 245792 | tf_op jit(solution)/shard_map/ppermute | solution.py:30
  50.1 2.9 %fusion = f32[384,1280]{1,0:T(8,128)S(1)} fusion(bf16[1280,1280]{1,0:T(8,128)(2,1)S(1)} %copy-done, bf16[96,1280]{1,0:T(8,128)(2,1)} %collective-permute-done.2, bf16[96,1280]{1,0:T(8,128)(2,1)} %collective-permute-done.1, bf16[96,1280]{1,0:T(8,128)(2,1)} %collective-permute-done, bf16[96,1280]{1,0:T(8,128)(2,1)S(1)} %bitcast.20), kind=kOutput, calls=%fused_computation | convolution fusion | flops 1262223360 | bytes 6225920 | tf_op jit(solution)/shard_map/dot_general | solution.py:20
  56.7 7.9 %collective-permute-done.10.rest_1_ = bf16[4,96,640]{2,1,0:T(8,128)(2,1)} collective-permute-done((bf16[4,96,640]{2,1,0:T(8,128)(2,1)}, bf16[4,96,640]{2,1,0:T(8,128)(2,1)}, u32[]{:S(2)}, u32[]{:S(2)}) %collective-permute-start.10) | collective-permute-done | bytes 491552 | tf_op jit(solution)/shard_map/ppermute | solution.py:30
  64.6 2.2 fusion.8
  71.5 18.7 %collective-permute-done.11.rest_2_ = bf16[4,96,640]{2,1,0:T(8,128)(2,1)} collective-permute-done((bf16[4,96,640]{2,1,0:T(8,128)(2,1)}, bf16[4,96,640]{2,1,0:T(8,128)(2,1)}, u32[]{:S(2)}, u32[]{:S(2)}) %collective-permute-start.11) | collective-permute-done | bytes 491552 | tf_op jit(solution)/shard_map/ppermute | solution.py:30
  91.3 2.4 add_convert_fusion
  96.0 2.5 %collective-permute-start.17 = (s32[6]{0:T(128)S(1)}, s32[6]{0:T(128)S(1)}, u32[]{:S(2)}, u32[]{:S(2)}) collective-permute-start(s32[6]{0:T(128)S(1)} %copy-done.8), channel_id=1, source_target_pairs={{0,4},{4,8},{8,12},{12,0},{1,5},{5,9},{9,13},{13,1},{2,6},{6,10},{... | collective-permute-start | bytes 80 | tf_op jit(solution)/shard_map/ppermute | solution.py:30
  98.5 4.7 %copy-done.1 = f32[1280,4,640]{2,1,0:T(4,128)S(1)} copy-done((f32[1280,4,640]{2,1,0:T(4,128)S(1)}, f32[1280,4,640]{2,1,0:T(4,128)}, u32[]{:S(2)}) %copy-start.1) | copy-done | bytes 13107224
  103.3 11.5 %weights.1.w = f32[5120,640]{1,0:T(8,128)S(1)} custom-call(f32[1280,4,640]{2,1,0:T(4,128)S(1)} %copy-done.1), custom_call_target="tpu_custom_call" | custom-call | flops 13107200 | bytes 26214400 | tf_op jit(solution)/shard_map/weights/pallas_call | solution.py:67
  114.8 4.7 %copy-done.2 = f32[5120,640]{1,0:T(8,128)} copy-done((f32[5120,640]{1,0:T(8,128)}, f32[5120,640]{1,0:T(8,128)S(1)}, u32[]{:S(2)}) %copy-start.2) | copy-done | bytes 13107224
  119.6 2.5 %collective-permute-start.18 = (s32[6]{0:T(128)S(1)}, s32[6]{0:T(128)S(1)}, u32[]{:S(2)}, u32[]{:S(2)}) collective-permute-start(s32[6]{0:T(128)S(1)} %collective-permute-done.17), channel_id=1, source_target_pairs={{0,4},{4,8},{8,12},{12,0},{1,5},{5,9},{9,13},{13,1},{2,6},{6,10},{... | collective-permute-start | bytes 80 | tf_op jit(solution)/shard_map/ppermute | solution.py:30
  122.0 2.9 %collective-permute-done.18 = s32[6]{0:T(128)S(1)} collective-permute-done((s32[6]{0:T(128)S(1)}, s32[6]{0:T(128)S(1)}, u32[]{:S(2)}, u32[]{:S(2)}) %collective-permute-start.18) | collective-permute-done | bytes 56 | tf_op jit(solution)/shard_map/ppermute | solution.py:30
  125.6 4.7 %collective-permute-done.19 = s32[6]{0:T(128)S(1)} collective-permute-done((s32[6]{0:T(128)S(1)}, s32[6]{0:T(128)S(1)}, u32[]{:S(2)}, u32[]{:S(2)}) %collective-permute-start.19) | collective-permute-done | bytes 56 | tf_op jit(solution)/shard_map/ppermute | solution.py:30
  131.4 2.3 maximum_select_fusion.1
  133.7 2.2 copy.13
  135.8 2.7 %maximum_select_fusion.ei = bf16[384,1280]{1,0:T(8,128)(2,1)} fusion(bf16[192,1280]{1,0:T(8,128)(2,1)} %collective-permute-done.5, bf16[192,1280]{1,0:T(8,128)(2,1)} %add_convert_fusion, pred[]{:T(512)S(6)} %eq.8), kind=kLoop, calls=%fused_computation.8 | loop fusion | flops 4423680 | bytes 1966081 | tf_op jit(solution)/shard_map/jit(_where)/select_n | solution.py:202
  138.6 44.1 %chunk_scores.3 = f32[16,24,128]{2,1,0:T(8,128)S(1)} custom-call(s32[1]{0:T(128)} %bitcast.idx, bf16[384,1280]{1,0:T(8,128)(2,1)} %maximum_select_fusion.ei, bf16[2,1280,128]{2,1,0:T(8,128)(2,1)} %bitcast.16, f32[5120,640]{1,0:T(8,128)} %copy-done.2, bf16[2,1280,640]{2,1,0:T(8,128)(2,1)} %all-gather.5.cloned.1.call-done.basis, ...), custom_call_target="tpu_custom_call" | custom-call | flops 33554432000 | bytes 12582912 | tf_op jit(solution)/shard_map/chunk_scores/pallas_call | solution.py:168
  182.7 44.3 %chunk_scores.2 = f32[16,24,128]{2,1,0:T(8,128)S(1)} custom-call(s32[1]{0:T(128)} %bitcast.idx, bf16[384,1280]{1,0:T(8,128)(2,1)} %maximum_select_fusion.ei, bf16[2,1280,128]{2,1,0:T(8,128)(2,1)} %bitcast.17, f32[5120,640]{1,0:T(8,128)} %copy-done.2, bf16[2,1280,640]{2,1,0:T(8,128)(2,1)} %all-gather.3.cloned.1.call-done.basis, ...), custom_call_target="tpu_custom_call" | custom-call | flops 33554432000 | bytes 12582912 | tf_op jit(solution)/shard_map/chunk_scores/pallas_call | solution.py:168
  232.8 3.6 %collective-permute-start.25 = (f32[16,6]{1,0:T(8,128)S(1)}, f32[16,6]{1,0:T(8,128)S(1)}, u32[]{:S(2)}, u32[]{:S(2)}) collective-permute-start(f32[16,6]{1,0:T(8,128)S(1)} %get-tuple-element.8), channel_id=1, source_target_pairs={{0,12},{4,0},{8,4},{12,8},{1,13},{5,1},{9,5},{13,9},{2,14},{6,2},{... | collective-permute-start | bytes 1160 | tf_op jit(solution)/shard_map/ppermute | solution.py:276
  (83 shorter events, 26.2 us)
Async XLA Ops:
  6.5 132.0 %all-gather.5.cloned.1.call-start = ((), (), s32[]{:S(2)}) async-start(), calls=%async_computation.1 | async-start | bytes 3686400 | tf_op jit(solution)/shard_map/all_gather | solution.py:243
  8.9 173.8 %all-gather.3.cloned.1.call-start = ((), (), s32[]{:S(2)}) async-start(), calls=%async_computation | async-start | bytes 3686400 | tf_op jit(solution)/shard_map/all_gather | solution.py:243
  8.9 11.2 %collective-permute-start = (bf16[96,1280]{1,0:T(8,128)(2,1)S(1)}, bf16[96,1280]{1,0:T(8,128)(2,1)}, u32[]{:S(2)}, u32[]{:S(2)}) collective-permute-start(bf16[96,1280]{1,0:T(8,128)(2,1)S(1)} %bitcast.19), channel_id=1, source_target_pairs={{0,4},{4,8},{8,12},{12,0},{1,5},{5,9},{9,13},{13,1},{2,6},{6,10},{... | collective-permute-start | bytes 737288 | tf_op jit(solution)/shard_map/ppermute | solution.py:30
  20.1 14.7 %collective-permute-start.1 = (bf16[96,1280]{1,0:T(8,128)(2,1)}, bf16[96,1280]{1,0:T(8,128)(2,1)}, u32[]{:S(2)}, u32[]{:S(2)}) collective-permute-start(bf16[96,1280]{1,0:T(8,128)(2,1)} %collective-permute-done), channel_id=1, source_target_pairs={{0,4},{4,8},{8,12},{12,0},{1,5},{5,9},{9,13},{13,1},{2,6},{6,10},{... | collective-permute-start | bytes 737288 | tf_op jit(solution)/shard_map/ppermute | solution.py:30
  34.8 15.3 %collective-permute-start.2 = (bf16[96,1280]{1,0:T(8,128)(2,1)}, bf16[96,1280]{1,0:T(8,128)(2,1)}, u32[]{:S(2)}, u32[]{:S(2)}) collective-permute-start(bf16[96,1280]{1,0:T(8,128)(2,1)} %collective-permute-done.1), channel_id=1, source_target_pairs={{0,4},{4,8},{8,12},{12,0},{1,5},{5,9},{9,13},{13,1},{2,6},{6,10},{... | collective-permute-start | bytes 737288 | tf_op jit(solution)/shard_map/ppermute | solution.py:30
  36.7 27.9 %collective-permute-start.10 = (bf16[4,96,640]{2,1,0:T(8,128)(2,1)}, bf16[4,96,640]{2,1,0:T(8,128)(2,1)}, u32[]{:S(2)}, u32[]{:S(2)}) collective-permute-start(bf16[4,96,640]{2,1,0:T(8,128)(2,1)} %bitcast.9.rest_0_), channel_id=1, source_target_pairs={{0,4},{4,8},{8,12},{12,0},{1,5},{5,9},{9,13},{13,1},{2,6},{6,10},{... | collective-permute-start | bytes 1474568 | tf_op jit(solution)/shard_map/ppermute | solution.py:30
  53.9 10.7 %collective-permute-start.3 = (bf16[192,1280]{1,0:T(8,128)(2,1)}, bf16[192,1280]{1,0:T(8,128)(2,1)}, u32[]{:S(2)}, u32[]{:S(2)}) collective-permute-start(bf16[192,1280]{1,0:T(8,128)(2,1)} %dynamic-slice_convert_fusion), channel_id=1, source_target_pairs={{0,1},{1,0},{2,3},{3,2},{4,5},{5,4},{6,7},{7,6},{8,9},{9,8},{10,11... | collective-permute-start | bytes 1474568 | tf_op jit(solution)/shard_map/ppermute | solution.py:24
  56.1 13.6 %collective-permute-start.6 = (bf16[128,1280]{1,0:T(8,128)(2,1)}, bf16[128,1280]{1,0:T(8,128)(2,1)}, u32[]{:S(2)}, u32[]{:S(2)}) collective-permute-start(bf16[128,1280]{1,0:T(8,128)(2,1)} %dynamic-slice_convert_fusion.1), channel_id=1, source_target_pairs={{0,1},{1,0},{2,3},{3,2},{4,5},{5,4},{6,7},{7,6},{8,9},{9,8},{10,11... | collective-permute-start | bytes 983048 | tf_op jit(solution)/shard_map/ppermute | solution.py:24
  64.6 25.6 %collective-permute-start.11 = (bf16[4,96,640]{2,1,0:T(8,128)(2,1)}, bf16[4,96,640]{2,1,0:T(8,128)(2,1)}, u32[]{:S(2)}, u32[]{:S(2)}) collective-permute-start(bf16[4,96,640]{2,1,0:T(8,128)(2,1)} %collective-permute-done.10.rest_1_), channel_id=1, source_target_pairs={{0,4},{4,8},{8,12},{12,0},{1,5},{5,9},{9,13},{13,1},{2,6},{6,10},{... | collective-permute-start | bytes 1474568 | tf_op jit(solution)/shard_map/ppermute | solution.py:30
  66.8 24.4 %collective-permute-start.4 = (bf16[192,1280]{1,0:T(8,128)(2,1)}, bf16[192,1280]{1,0:T(8,128)(2,1)}, u32[]{:S(2)}, u32[]{:S(2)}) collective-permute-start(bf16[192,1280]{1,0:T(8,128)(2,1)} %fusion.8), channel_id=1, source_target_pairs={{0,2},{2,0},{1,3},{3,1},{4,6},{6,4},{5,7},{7,5},{8,10},{10,8},{9,1... | collective-permute-start | bytes 1474568 | tf_op jit(solution)/shard_map/ppermute | solution.py:24
  69.7 68.8 %collective-permute-start.9 = (bf16[4,256,640]{2,1,0:T(8,128)(2,1)}, bf16[4,256,640]{2,1,0:T(8,128)(2,1)}, u32[]{:S(2)}, u32[]{:S(2)}) collective-permute-start(bf16[4,256,640]{2,1,0:T(8,128)(2,1)} %bitcast.6.q_own), channel_id=1, source_target_pairs={{0,1},{1,0},{2,3},{3,2},{4,5},{5,4},{6,7},{7,6},{8,9},{9,8},{10,11... | collective-permute-start | bytes 3932168 | tf_op jit(solution)/shard_map/ppermute | solution.py:24
  71.1 22.6 %collective-permute-start.7 = (bf16[128,1280]{1,0:T(8,128)(2,1)S(1)}, bf16[128,1280]{1,0:T(8,128)(2,1)S(1)}, u32[]{:S(2)}, u32[]{:S(2)}) collective-permute-start(bf16[128,1280]{1,0:T(8,128)(2,1)S(1)} %fusion.9), channel_id=1, source_target_pairs={{0,2},{2,0},{1,3},{3,1},{4,6},{6,4},{5,7},{7,5},{8,10},{10,8},{9,1... | collective-permute-start | bytes 983048 | tf_op jit(solution)/shard_map/ppermute | solution.py:24
  90.2 40.6 %collective-permute-start.12 = (bf16[4,96,640]{2,1,0:T(8,128)(2,1)}, bf16[4,96,640]{2,1,0:T(8,128)(2,1)}, u32[]{:S(2)}, u32[]{:S(2)}) collective-permute-start(bf16[4,96,640]{2,1,0:T(8,128)(2,1)} %collective-permute-done.11.rest_2_), channel_id=1, source_target_pairs={{0,4},{4,8},{8,12},{12,0},{1,5},{5,9},{9,13},{13,1},{2,6},{6,10},{... | collective-permute-start | bytes 1474568 | tf_op jit(solution)/shard_map/ppermute | solution.py:30
  93.7 37.2 %collective-permute-start.5 = (bf16[192,1280]{1,0:T(8,128)(2,1)}, bf16[192,1280]{1,0:T(8,128)(2,1)}, u32[]{:S(2)}, u32[]{:S(2)}) collective-permute-start(bf16[192,1280]{1,0:T(8,128)(2,1)} %add_convert_fusion), channel_id=1, source_target_pairs={{0,1},{1,0},{2,3},{3,2},{4,5},{5,4},{6,7},{7,6},{8,9},{9,8},{10,11... | collective-permute-start | bytes 1474568 | tf_op jit(solution)/shard_map/ppermute | solution.py:24
  95.5 34.8 %collective-permute-start.8 = (bf16[128,1280]{1,0:T(8,128)(2,1)}, bf16[128,1280]{1,0:T(8,128)(2,1)}, u32[]{:S(2)}, u32[]{:S(2)}) collective-permute-start(bf16[128,1280]{1,0:T(8,128)(2,1)} %add_convert_fusion.1), channel_id=1, source_target_pairs={{0,1},{1,0},{2,3},{3,2},{4,5},{5,4},{6,7},{7,6},{8,9},{9,8},{10,11... | collective-permute-start | bytes 983048 | tf_op jit(solution)/shard_map/ppermute | solution.py:24
  96.0 23.5 %collective-permute-start.17 = (s32[6]{0:T(128)S(1)}, s32[6]{0:T(128)S(1)}, u32[]{:S(2)}, u32[]{:S(2)}) collective-permute-start(s32[6]{0:T(128)S(1)} %copy-done.8), channel_id=1, source_target_pairs={{0,4},{4,8},{8,12},{12,0},{1,5},{5,9},{9,13},{13,1},{2,6},{6,10},{... | collective-permute-start | bytes 80 | tf_op jit(solution)/shard_map/ppermute | solution.py:30
  124.9 5.3 %collective-permute-start.19 = (s32[6]{0:T(128)S(1)}, s32[6]{0:T(128)S(1)}, u32[]{:S(2)}, u32[]{:S(2)}) collective-permute-start(s32[6]{0:T(128)S(1)} %collective-permute-done.18), channel_id=1, source_target_pairs={{0,4},{4,8},{8,12},{12,0},{1,5},{5,9},{9,13},{13,1},{2,6},{6,10},{... | collective-permute-start | bytes 80 | tf_op jit(solution)/shard_map/ppermute | solution.py:30
  130.2 8.3 %collective-permute-start.13 = (bf16[4,96,640]{2,1,0:T(8,128)(2,1)}, bf16[4,96,640]{2,1,0:T(8,128)(2,1)}, u32[]{:S(2)}, u32[]{:S(2)}) collective-permute-start(bf16[4,96,640]{2,1,0:T(8,128)(2,1)} %bitcast.9.rest_0_), channel_id=1, source_target_pairs={{0,1},{1,0},{2,3},{3,2},{4,5},{5,4},{6,7},{7,6},{8,9},{9,8},{10,11... | collective-permute-start | bytes 1474568 | tf_op jit(solution)/shard_map/ppermute | solution.py:24
  130.3 8.2 %collective-permute-start.14 = (bf16[4,96,640]{2,1,0:T(8,128)(2,1)}, bf16[4,96,640]{2,1,0:T(8,128)(2,1)}, u32[]{:S(2)}, u32[]{:S(2)}) collective-permute-start(bf16[4,96,640]{2,1,0:T(8,128)(2,1)} %collective-permute-done.10.rest_1_), channel_id=1, source_target_pairs={{0,1},{1,0},{2,3},{3,2},{4,5},{5,4},{6,7},{7,6},{8,9},{9,8},{10,11... | collective-permute-start | bytes 1474568 | tf_op jit(solution)/shard_map/ppermute | solution.py:24
  130.8 7.7 %collective-permute-start.15 = (bf16[4,96,640]{2,1,0:T(8,128)(2,1)}, bf16[4,96,640]{2,1,0:T(8,128)(2,1)}, u32[]{:S(2)}, u32[]{:S(2)}) collective-permute-start(bf16[4,96,640]{2,1,0:T(8,128)(2,1)} %collective-permute-done.11.rest_2_), channel_id=1, source_target_pairs={{0,1},{1,0},{2,3},{3,2},{4,5},{5,4},{6,7},{7,6},{8,9},{9,8},{10,11... | collective-permute-start | bytes 1474568 | tf_op jit(solution)/shard_map/ppermute | solution.py:24
  130.9 7.6 %collective-permute-start.16 = (bf16[4,96,640]{2,1,0:T(8,128)(2,1)}, bf16[4,96,640]{2,1,0:T(8,128)(2,1)}, u32[]{:S(2)}, u32[]{:S(2)}) collective-permute-start(bf16[4,96,640]{2,1,0:T(8,128)(2,1)} %collective-permute-done.12.rest_3_), channel_id=1, source_target_pairs={{0,1},{1,0},{2,3},{3,2},{4,5},{5,4},{6,7},{7,6},{8,9},{9,8},{10,11... | collective-permute-start | bytes 1474568 | tf_op jit(solution)/shard_map/ppermute | solution.py:24
  232.5 5.5 %collective-permute-start.23 = (f32[16,6]{1,0:T(8,128)S(1)}, f32[16,6]{1,0:T(8,128)S(1)}, u32[]{:S(2)}, u32[]{:S(2)}) collective-permute-start(f32[16,6]{1,0:T(8,128)S(1)} %get-tuple-element.7), channel_id=1, source_target_pairs={{0,4},{4,8},{8,12},{12,0},{1,5},{5,9},{9,13},{13,1},{2,6},{6,10},{... | collective-permute-start | bytes 1160 | tf_op jit(solution)/shard_map/ppermute | solution.py:276
  232.5 5.4 %collective-permute-start.24 = (f32[16,6]{1,0:T(8,128)S(1)}, f32[16,6]{1,0:T(8,128)S(1)}, u32[]{:S(2)}, u32[]{:S(2)}) collective-permute-start(f32[16,6]{1,0:T(8,128)S(1)} %get-tuple-element.9), channel_id=1, source_target_pairs={{0,8},{4,12},{8,0},{12,4},{1,9},{5,13},{9,1},{13,5},{2,10},{6,14},... | collective-permute-start | bytes 1160 | tf_op jit(solution)/shard_map/ppermute | solution.py:276
  232.8 5.8 %collective-permute-start.25 = (f32[16,6]{1,0:T(8,128)S(1)}, f32[16,6]{1,0:T(8,128)S(1)}, u32[]{:S(2)}, u32[]{:S(2)}) collective-permute-start(f32[16,6]{1,0:T(8,128)S(1)} %get-tuple-element.8), channel_id=1, source_target_pairs={{0,12},{4,0},{8,4},{12,8},{1,13},{5,1},{9,5},{13,9},{2,14},{6,2},{... | collective-permute-start | bytes 1160 | tf_op jit(solution)/shard_map/ppermute | solution.py:276
  (15 other events, 162.4 us)
Sparse Core Ops, SparseCore 0:
  9.6 87.4 all-gather.4
  99.2 60.0 all-gather.2
where the time goes:
time: 247 us; the launch traced here: 246 us
  Pallas kernels  99.9 us (40%)
  waiting for transfers between devices  70 us (28%)
  starting transfers between devices  23.4 us (9%)
  local copies, waits for them, and re-layouts  20 us (8%)
  other arithmetic  15.1 us (6%)
  between operations  13.6 us (6%)
  matrix products  4.11 us (2%)
    pallas_call x2, Pallas kernels, chunk_scores(): pl.pallas_call(functools.partial(score_kernel, n, q_count, seq, first), o...  88.4 us
    ppermute x9, waiting for transfers between devices, ring(): lax.ppermute(parts[-1], 'dp', [(i, (i + 1) % n) for i in range(n)])  64.7 us
    ppermute x9, starting transfers between devices, ring(): lax.ppermute(parts[-1], 'dp', [(i, (i + 1) % n) for i in range(n)])  13.4 us
    unnamed x24, local copies, waits for them, and re-layouts  12.9 us
    pallas_call x1, Pallas kernels, weights(): pl.pallas_call(functools.partial(weight_kernel, blocks, step), grid=(bloc...  11.5 us
    select_n x2, other arithmetic, sum_features(): jnp.where(sub == 0, jnp.concatenate([total, rest], 0), jnp.concatenate([r...  4.99 us
  transfers between devices with their start and end apart: 28, of which 11 were waited for; matrix products, arithmetic and copies ran while one was open for 11% of the time, Pallas kernels for 23%

commit v1 on v0

--- a/solution.py
+++ b/solution.py
@@ -24,10 +24,14 @@
     return lax.ppermute(x, axis, [(0, 1), (1, 0)])
 
 
+def step_along(x, n):
+    return lax.ppermute(x, "dp", [(i, (i + 1) % n) for i in range(n)])
+
+
 def ring(x, n):
     parts = [x]
     for _ in range(n - 1):
-        parts.append(lax.ppermute(parts[-1], "dp", [(i, (i + 1) % n) for i in range(n)]))
+        parts.append(step_along(parts[-1], n))
     return parts
 
 
@@ -71,7 +75,7 @@
         in_specs=[ANY],
         out_specs=pl.BlockSpec((step, width), lambda i: (i, 0)),
         scratch_shapes=[pltpu.VMEM((2, step, width), F32), pltpu.SemaphoreType.DMA((2,))],
-        compiler_params=pltpu.CompilerParams(vmem_limit_bytes=24 * MIB),
+        compiler_params=pltpu.CompilerParams(vmem_limit_bytes=58 * MIB),
         cost_estimate=pl.CostEstimate(
             flops=4 * lam.size, bytes_accessed=8 * lam.size, transcendentals=0
         ),
@@ -79,13 +83,14 @@
     )(lam)
 
 
-def score_kernel(n, q_count, seq, first, idx, ei, qit, w, basis, q_own, q_oth, *rest):
-    xs, zs, rest = rest[:n], rest[n : 2 * n], rest[2 * n :]
+def score_kernel(n, q_count, seq, first, parts, idx, ei, qit, w, q_own, q_oth, *rest):
+    e_own, e_oth, rest = rest[:parts], rest[parts : 2 * parts], rest[2 * parts :]
+    halves, rest = rest[:-11], rest[-11:]
     out, full, tok_own, tok_oth, hid, wv, p0, p1, acc, sems, w_sem = rest
-    sub = idx[0]
+    sub, grp, dpi = idx[0], idx[1], idx[2]
     chunk, all_rows, width = full.shape
     half_rows = all_rows // 2
-    q_rows, e_rows = q_own.shape[1], xs[0].shape[1]
+    q_rows, e_rows = q_own.shape[1], e_own[0].shape[1] * parts // n
     j_rows = ei.shape[1]
     ex_count = ei.shape[0] // seq
     per = 128 // seq
@@ -94,12 +99,21 @@
     moves, w_moves = [], []
     for j in range(chunk):
         b = first + j
-        moves.append((basis.at[j], full.at[j]))
-        for own, oth, at, size in [(q_own, q_oth, 0, q_rows)] + [
-            (xs[k], zs[k], q_rows + k * e_rows, e_rows) for k in range(n)
-        ]:
-            moves.append((own.at[b], tok_own.at[j, pl.ds(at, size), :]))
-            moves.append((oth.at[b], tok_oth.at[j, pl.ds(at, size), :]))
+        piece = all_rows // n // len(halves)
+        for h, half in enumerate(halves):
+            shift = (grp if h == 0 else 1 - grp) * piece if len(halves) == 2 else 0
+            for k in range(n):
+                to = pl.ds(pl.multiple_of(k * piece * len(halves) + shift, 16), piece)
+                moves.append((half.at[j, pl.ds(k * piece, piece), :], full.at[j, to, :]))
+        moves.append((q_own.at[b], tok_own.at[j, pl.ds(0, q_rows), :]))
+        moves.append((q_oth.at[b], tok_oth.at[j, pl.ds(0, q_rows), :]))
+        for k in range(n):
+            to = pl.ds(q_rows + k * e_rows, e_rows)
+            part = k if parts == n else 0
+            at = 0 if parts == n else pl.multiple_of(lax.rem(dpi + n - k, n) * e_rows, 16)
+            rows = pl.ds(at, e_rows)
+            moves.append((e_own[part].at[j, rows, :], tok_own.at[j, to, :]))
+            moves.append((e_oth[part].at[j, rows, :], tok_oth.at[j, to, :]))
         w_moves.append((w.at[pl.ds(b * j_rows, j_rows), :], wv.at[:, pl.ds(j * width, width)]))
     copies = [pltpu.make_async_copy(a, c, sems.at[i]) for i, (a, c) in enumerate(moves)]
     w_copies = [pltpu.make_async_copy(a, c, w_sem.at[i]) for i, (a, c) in enumerate(w_moves)]
@@ -116,7 +130,7 @@
     for copy in w_copies:
         copy.wait()
 
-    m_step = j_rows // 2
+    m_step = j_rows
     tiles = [(at, min(256, columns - at)) for at in range(0, columns, 256)]
 
     def outer(q, dst, at, size):
@@ -158,17 +172,18 @@
     out[...] = acc[...].sum(2)
 
 
-def chunk_scores(n, q_count, seq, first, idx, ei, qit, w, basis, q_own, q_oth, xs, zs):
-    chunk, all_rows, width = basis.shape
+def chunk_scores(n, q_count, seq, first, idx, ei, qit, w, q_own, q_oth, xs, zs, halves):
+    chunk, _, width = halves[0].shape
+    all_rows = halves[0].shape[1] * len(halves)
     ex_rows, j_rows = ei.shape
     q_rows = q_own.shape[1]
     ex_count = ex_rows // seq
     tokens = pltpu.VMEM((chunk, q_rows + ex_rows, width), BF)
     flops = 2 * q_count * j_rows * chunk * width * (256 + ex_rows)
     return pl.pallas_call(
-        functools.partial(score_kernel, n, q_count, seq, first),
+        functools.partial(score_kernel, n, q_count, seq, first, len(xs)),
         out_shape=jax.ShapeDtypeStruct((q_count, ex_count, 128), F32),
-        in_specs=[SMEM, VMEM, VMEM] + [ANY] * (4 + 2 * n),
+        in_specs=[SMEM, VMEM, VMEM] + [ANY] * (3 + 2 * len(xs) + len(halves)),
         out_specs=VMEM,
         scratch_shapes=[
             pltpu.VMEM((chunk, all_rows, width), BF),
@@ -179,13 +194,13 @@
             pltpu.VMEM((j_rows, chunk * width), BF),
             pltpu.VMEM((j_rows, chunk * width), BF),
             pltpu.VMEM((q_count, ex_count, 8, 128), F32),
-            pltpu.SemaphoreType.DMA((chunk * (3 + 2 * n),)),
+            pltpu.SemaphoreType.DMA((chunk * (2 + 2 * n + len(halves) * n),)),
             pltpu.SemaphoreType.DMA((chunk,)),
         ],
-        compiler_params=pltpu.CompilerParams(vmem_limit_bytes=52 * MIB),
+        compiler_params=pltpu.CompilerParams(vmem_limit_bytes=58 * MIB),
         cost_estimate=pl.CostEstimate(flops=flops, bytes_accessed=12 * MIB, transcendentals=0),
         name="chunk_scores",
-    )(idx, ei, qit, w, basis, q_own, q_oth, *xs, *zs)
+    )(idx, ei, qit, w, q_own, q_oth, *xs, *zs, *halves)
 
 
 def sum_features(part, sub, sizes):
@@ -224,37 +239,57 @@
     j_rows = input_basis.shape[1]
     e_rows, q_rows = ex_count * seq, q_count * q_seq
     share = sizes["groups"] == 2 and rows % 32 == 0
-    idx = sub.astype(jnp.int32).reshape(1)
-
-    acts = ring(ex_acts.reshape(e_rows, input_cols), n)
-    keep = ex_mask.astype(BF).reshape(e_rows, 1, 1)
-    e_raw = jnp.transpose(ex_grads.reshape(e_rows, blocks, width) * keep, (1, 0, 2))
-    q_raw = jnp.transpose(query_grads.reshape(q_rows, blocks, width), (1, 0, 2))
-    xs = ring(e_raw, n)
-    zs = [swap(x, "sub") for x in xs]
-    q_oth = swap(q_raw, "sub")
-    all_ids = jnp.concatenate(ring(ex_ids, n))
+    idx = jnp.stack([sub, grp, dpi]).astype(jnp.int32)
 
     chunk = 2 if blocks % 2 == 0 else 1
     mine = hidden_basis
     if share:
         mine = lax.dynamic_slice_in_dim(hidden_basis, grp * (rows // 2), rows // 2, 1)
-    full = [
-        lax.all_gather(
-            mine[b : b + chunk], ("dp", "groups") if share else "dp", axis=1, tiled=True
-        )
+    lam, mine = lax.optimization_barrier((eigenvalues, mine))
+    halves = [
+        lax.all_gather(mine[b : b + chunk], "dp", axis=1, tiled=True)
         for b in range(0, blocks, chunk)
     ]
 
+    keep = ex_mask.astype(BF).reshape(e_rows, 1, 1)
+    e_raw = jnp.transpose(ex_grads.reshape(e_rows, blocks, width) * keep, (1, 0, 2))
+    q_raw = jnp.transpose(query_grads.reshape(q_rows, blocks, width), (1, 0, 2))
+    q_oth = swap(q_raw, "sub")
+
+    w = weights(lam)
+    travel = [(ex_acts.reshape(e_rows, input_cols), ex_ids, e_raw[:chunk])]
+    for k in range(1, n):
+        last = [step_along(x, n) for x in travel[-1]]
+        if k == 1:
+            *last, w = lax.optimization_barrier((*last, w))
+        elif k == 2:
+            *last, halves[0] = lax.optimization_barrier((*last, halves[0]))
+        else:
+            last = lax.optimization_barrier(last)
+        travel.append(last)
+    acts, ids, first = zip(*travel)
+    all_ids = jnp.concatenate(ids)
+    xs = [list(first)]
+    zs = [[swap(x, "sub") for x in first]]
+
     q_in = sum_features(dot(query_acts.reshape(q_rows, input_cols), input_basis), sub, sizes)
     qit = jnp.transpose(q_in.reshape(q_rows // 128, 128, j_rows), (0, 2, 1))
-    w = weights(eigenvalues)
     ei = sum_features(dot(jnp.concatenate(acts, 0), input_basis), sub, sizes)
 
+    others = [swap(half, "groups") if share else None for half in halves]
     total = 0.0
-    for i, basis in enumerate(full):
+    for i in range(blocks // chunk):
+        if i > 0:
+            later, halves[i] = lax.optimization_barrier(
+                (e_raw[i * chunk : (i + 1) * chunk], halves[i])
+            )
+            later = lax.all_gather(later, "dp", axis=1, tiled=True)
+            later, total = lax.optimization_barrier((later, total))
+            xs.append([later])
+            zs.append([swap(later, "sub")])
+        rows_here = [halves[i], others[i]] if share else [halves[i]]
         total = total + chunk_scores(
-            n, q_count, seq, i * chunk, idx, ei, qit, w, basis, q_raw, q_oth, xs, zs
+            n, q_count, seq, i * chunk, idx, ei, qit, w, q_raw, q_oth, xs[i], zs[i], rows_here
         )
     scores = total.sum(2)
 

time: 247 us -> 258 us (1.045)
  waiting for transfers between devices: 70 us -> 45.9 us
  blocking collectives: 0 us -> 20.6 us
  starting transfers between devices: 23.4 us -> 34.1 us
  Pallas kernels: 99.9 us -> 107 us
  local copies, waits for them, and re-layouts: 20 us -> 14.7 us
    ppermute x9, waiting for transfers between devices: 64.7 us -> 24.9 us  [step_along(): return lax.ppermute(x, 'dp', [(i, (i + 1) % n) for i in range(n)])]
    all_gather x0 -> x1, blocking collectives: none -> 20.6 us  [shards(): later = lax.all_gather(later, 'dp', axis=1, tiled=True)]
    ppermute x11 -> x14, waiting for transfers between devices: 0.03 us -> 16 us  [swap(): return lax.ppermute(x, axis, [(0, 1), (1, 0)])]
    ppermute x9, starting transfers between devices: 13.4 us -> 21.7 us  [step_along(): return lax.ppermute(x, 'dp', [(i, (i + 1) % n) for i in range(n)])]
    unnamed x24, local copies, waits for them, and re-layouts: 12.9 us -> 5.87 us
    pallas_call x1, Pallas kernels: 11.5 us -> 16.2 us  [weights(): pl.pallas_call(functools.partial(weight_kernel, blocks, step), grid=(bloc...]
    ppermute x11 -> x14, starting transfers between devices: 4.12 us -> 6.66 us  [swap(): return lax.ppermute(x, axis, [(0, 1), (1, 0)])]
  transfers between devices with their start and end apart: 28 -> 31, of which waited for: 11 -> 10; matrix products, arithmetic and copies ran while one was open for 11% -> 11% of each run, Pallas kernels for 23% -> 24%
where the time goes in v1:
time: 258 us; the launch traced here: 257 us
  Pallas kernels  107 us (41%)
  waiting for transfers between devices  45.9 us (18%)
  starting transfers between devices  34.1 us (13%)
  blocking collectives  20.6 us (8%)
  other arithmetic  14.9 us (6%)
  local copies, waits for them, and re-layouts  14.7 us (6%)
  between operations  13.6 us (5%)
  matrix products  6.16 us (2%)
    pallas_call x2, Pallas kernels, chunk_scores(): pl.pallas_call(functools.partial(score_kernel, n, q_count, seq, first, le...  90.6 us
    ppermute x9, waiting for transfers between devices, step_along(): return lax.ppermute(x, 'dp', [(i, (i + 1) % n) for i in range(n)])  24.9 us
    ppermute x9, starting transfers between devices, step_along(): return lax.ppermute(x, 'dp', [(i, (i + 1) % n) for i in range(n)])  21.7 us
    all_gather x1, blocking collectives, shards(): later = lax.all_gather(later, 'dp', axis=1, tiled=True)  20.6 us
    pallas_call x1, Pallas kernels, weights(): pl.pallas_call(functools.partial(weight_kernel, blocks, step), grid=(bloc...  16.2 us
    ppermute x14, waiting for transfers between devices, swap(): return lax.ppermute(x, axis, [(0, 1), (1, 0)])  16 us
    ppermute x14, starting transfers between devices, swap(): return lax.ppermute(x, axis, [(0, 1), (1, 0)])  6.66 us
    dot_general x2, matrix products, dot(): return jnp.dot(a, b, preferred_element_type=F32)  5.97 us
  transfers between devices with their start and end apart: 31, of which 10 were waited for; matrix products, arithmetic and copies ran while one was open for 11% of the time, Pallas kernels for 24%

profile of v1, /device:TPU:0, one launch (start us, length us, event | category | flops | bytes accessed | tf_op | source)
XLA Modules:
  0.0 256.8 jit_solution(7559218504550700276)
XLA Ops:
  9.0 1.9 copy.13
  12.9 3.0 %collective-permute-start.2 = (bf16[2,96,640]{2,1,0:T(8,128)(2,1)}, bf16[2,96,640]{2,1,0:T(8,128)(2,1)S(1)}, u32[]{:S(2)}, u32[]{:S(2)}) collective-permute-start(bf16[2,96,640]{2,1,0:T(8,128)(2,1)} %get-tuple-element.41.rest_0_), channel_id=1, source_target_pairs={{0,4},{4,8},{8,12},{12,0},{1,5},{5,9},{9,13},{13,1},{2,6},{6,10},{... | collective-permute-start | bytes 737288 | tf_op jit(solution)/shard_map/ppermute | solution.py:28
  19.0 16.2 %weights.1.w = f32[5120,640]{1,0:T(8,128)} custom-call(f32[1280,4,640]{2,1,0:T(4,128)} %lam), custom_call_target="tpu_custom_call" | custom-call | flops 13107200 | bytes 26214400 | tf_op jit(solution)/shard_map/weights/pallas_call | solution.py:71
  35.7 7.3 %collective-permute-start.5 = (bf16[2,96,640]{2,1,0:T(8,128)(2,1)S(1)}, bf16[2,96,640]{2,1,0:T(8,128)(2,1)S(1)}, u32[]{:S(2)}, u32[]{:S(2)}) collective-permute-start(bf16[2,96,640]{2,1,0:T(8,128)(2,1)S(1)} %collective-permute-done.2.rest_1_), channel_id=1, source_target_pairs={{0,4},{4,8},{8,12},{12,0},{1,5},{5,9},{9,13},{13,1},{2,6},{6,10},{... | collective-permute-start | bytes 737288 | tf_op jit(solution)/shard_map/ppermute | solution.py:28
  42.9 2.5 collective-permute-start.3
  45.4 3.1 %collective-permute-start.4 = (s32[6]{0:T(128)S(1)}, s32[6]{0:T(128)S(1)}, u32[]{:S(2)}, u32[]{:S(2)}) collective-permute-start(s32[6]{0:T(128)S(1)} %collective-permute-done.1), channel_id=1, source_target_pairs={{0,4},{4,8},{8,12},{12,0},{1,5},{5,9},{9,13},{13,1},{2,6},{6,10},{... | collective-permute-start | bytes 80 | tf_op jit(solution)/shard_map/ppermute | solution.py:28
  48.5 18.0 %collective-permute-done.4 = s32[6]{0:T(128)S(1)} collective-permute-done((s32[6]{0:T(128)S(1)}, s32[6]{0:T(128)S(1)}, u32[]{:S(2)}, u32[]{:S(2)}) %collective-permute-start.4) | collective-permute-done | bytes 56 | tf_op jit(solution)/shard_map/ppermute | solution.py:28
  68.3 3.2 %fusion.15 = f32[256,1280]{1,0:T(8,128)} fusion(bf16[256,1280]{1,0:T(8,128)(2,1)} %bitcast.21, bf16[1280,1280]{1,0:T(8,128)(2,1)S(1)} %copy-done), kind=kOutput, calls=%fused_computation.34 | convolution fusion | flops 838860800 | bytes 5242880 | tf_op jit(solution)/shard_map/dot_general | solution.py:20
  71.5 1.9 dynamic-slice_convert_fusion.1
  75.0 6.4 %collective-permute-done.7 = s32[6]{0:T(128)S(1)} collective-permute-done((s32[6]{0:T(128)S(1)}, s32[6]{0:T(128)S(1)}, u32[]{:S(2)}, u32[]{:S(2)}) %collective-permute-start.7) | collective-permute-done | bytes 56 | tf_op jit(solution)/shard_map/ppermute | solution.py:28
  81.5 2.8 %fusion = f32[384,1280]{1,0:T(8,128)S(1)} fusion(bf16[1280,1280]{1,0:T(8,128)(2,1)S(1)} %copy-done, bf16[96,1280]{1,0:T(8,128)(2,1)} %collective-permute-done.6, bf16[96,1280]{1,0:T(8,128)(2,1)} %collective-permute-done.3, bf16[96,1280]{1,0:T(8,128)(2,1)} %copy-done.8, bf16[96,1280]{1,0:T(8,128)(2,1)} %bitcast.23), kind=kOutput, calls=%fused_computation | convolution fusion | flops 1262223360 | bytes 6225920 | tf_op jit(solution)/shard_map/dot_general | solution.py:20
  88.2 2.0 fusion.9
  91.7 2.3 fusion.8
  95.1 5.9 %collective-permute-done.13 = bf16[128,1280]{1,0:T(8,128)(2,1)} collective-permute-done((bf16[128,1280]{1,0:T(8,128)(2,1)}, bf16[128,1280]{1,0:T(8,128)(2,1)}, u32[]{:S(2)}, u32[]{:S(2)}) %collective-permute-start.13) | collective-permute-done | bytes 327712 | tf_op jit(solution)/shard_map/ppermute | solution.py:24
  103.9 7.2 %collective-permute-done.10 = bf16[192,1280]{1,0:T(8,128)(2,1)} collective-permute-done((bf16[192,1280]{1,0:T(8,128)(2,1)}, bf16[192,1280]{1,0:T(8,128)(2,1)}, u32[]{:S(2)}, u32[]{:S(2)}) %collective-permute-start.10) | collective-permute-done | bytes 491552 | tf_op jit(solution)/shard_map/ppermute | solution.py:24
  111.2 2.5 add_convert_fusion
  115.1 2.2 copy.14
  117.3 20.6 %all_gather.10.rest_0_ = bf16[2,384,640]{2,1,0:T(8,128)(2,1)} all-gather(bf16[2,96,640]{2,1,0:T(8,128)(2,1)S(1)} %get-tuple-element.23), channel_id=1, replica_groups=mesh['groups'=2,'dp'=4,'owner'=2,'sub'=2] {'dp'}, dimensions={1}, use_global_device_ids=true | all-gather | bytes 1228800 | tf_op jit(solution)/shard_map/all_gather | solution.py:286
  138.4 2.7 %maximum_select_fusion.ei = bf16[384,1280]{1,0:T(8,128)(2,1)} fusion(bf16[192,1280]{1,0:T(8,128)(2,1)} %collective-permute-done.11, bf16[192,1280]{1,0:T(8,128)(2,1)} %add_convert_fusion, pred[]{:T(512)S(6)} %eq.8), kind=kLoop, calls=%fused_computation.8 | loop fusion | flops 4423680 | bytes 1966081 | tf_op jit(solution)/shard_map/jit(_where)/select_n | solution.py:217
  143.5 44.8 %chunk_scores.2 = f32[16,24,128]{2,1,0:T(8,128)} custom-call(s32[3]{0:T(128)} %pad_add_fusion.idx, bf16[384,1280]{1,0:T(8,128)(2,1)} %maximum_select_fusion.ei, bf16[2,1280,128]{2,1,0:T(8,128)(2,1)} %bitcast.19, f32[5120,640]{1,0:T(8,128)} %weights.1.w, bf16[4,256,640]{2,1,0:T(8,128)(2,1)} %bitcast.10.q_own, ...), custom_call_target="tpu_custom_call" | custom-call | flops 33554432000 | bytes 12582912 | tf_op jit(solution)/shard_map/chunk_scores/pallas_call | solution.py:183
  188.5 2.8 %collective-permute-done.21.rest_1_ = bf16[2,384,640]{2,1,0:T(8,128)(2,1)} collective-permute-done((bf16[2,384,640]{2,1,0:T(8,128)(2,1)}, bf16[2,384,640]{2,1,0:T(8,128)(2,1)}, u32[]{:S(2)}, u32[]{:S(2)}) %collective-permute-start.21) | collective-permute-done | bytes 983072 | tf_op jit(solution)/shard_map/ppermute | solution.py:24
  191.3 45.8 %chunk_scores.3 = f32[16,24,128]{2,1,0:T(8,128)} custom-call(s32[3]{0:T(128)} %pad_add_fusion.idx, bf16[384,1280]{1,0:T(8,128)(2,1)} %maximum_select_fusion.ei, bf16[2,1280,128]{2,1,0:T(8,128)(2,1)} %bitcast.20, f32[5120,640]{1,0:T(8,128)} %weights.1.w, bf16[4,256,640]{2,1,0:T(8,128)(2,1)} %bitcast.10.q_own, ...), custom_call_target="tpu_custom_call" | custom-call | flops 33554432000 | bytes 12582912 | tf_op jit(solution)/shard_map/chunk_scores/pallas_call | solution.py:183
  240.2 1.9 collective-permute-done.24
  243.2 2.3 collective-permute-start.27
  (93 shorter events, 34.0 us)
Async XLA Ops:
  6.5 60.7 %all-gather.5.cloned.1.call-start = ((), (), s32[]{:S(2)}) async-start(), calls=%async_computation.1 | async-start | bytes 2048000 | tf_op jit(solution)/shard_map/all_gather | solution.py:250
  8.9 108.4 %all-gather.3.cloned.1.call-start = ((), (), s32[]{:S(2)}) async-start(), calls=%async_computation | async-start | bytes 2048000 | tf_op jit(solution)/shard_map/all_gather | solution.py:250
  12.9 22.8 %collective-permute-start.2 = (bf16[2,96,640]{2,1,0:T(8,128)(2,1)}, bf16[2,96,640]{2,1,0:T(8,128)(2,1)S(1)}, u32[]{:S(2)}, u32[]{:S(2)}) collective-permute-start(bf16[2,96,640]{2,1,0:T(8,128)(2,1)} %get-tuple-element.41.rest_0_), channel_id=1, source_target_pairs={{0,4},{4,8},{8,12},{12,0},{1,5},{5,9},{9,13},{13,1},{2,6},{6,10},{... | collective-permute-start | bytes 737288 | tf_op jit(solution)/shard_map/ppermute | solution.py:28
  15.9 19.8 %collective-permute-start = (bf16[96,1280]{1,0:T(8,128)(2,1)}, bf16[96,1280]{1,0:T(8,128)(2,1)S(1)}, u32[]{:S(2)}, u32[]{:S(2)}) collective-permute-start(bf16[96,1280]{1,0:T(8,128)(2,1)} %bitcast.22), channel_id=1, source_target_pairs={{0,4},{4,8},{8,12},{12,0},{1,5},{5,9},{9,13},{13,1},{2,6},{6,10},{... | collective-permute-start | bytes 737288 | tf_op jit(solution)/shard_map/ppermute | solution.py:28
  17.5 18.2 %collective-permute-start.1 = (s32[6]{0:T(128)S(1)}, s32[6]{0:T(128)S(1)}, u32[]{:S(2)}, u32[]{:S(2)}) collective-permute-start(s32[6]{0:T(128)S(1)} %copy-done.5), channel_id=1, source_target_pairs={{0,4},{4,8},{8,12},{12,0},{1,5},{5,9},{9,13},{13,1},{2,6},{6,10},{... | collective-permute-start | bytes 80 | tf_op jit(solution)/shard_map/ppermute | solution.py:28
  35.7 30.9 %collective-permute-start.5 = (bf16[2,96,640]{2,1,0:T(8,128)(2,1)S(1)}, bf16[2,96,640]{2,1,0:T(8,128)(2,1)S(1)}, u32[]{:S(2)}, u32[]{:S(2)}) collective-permute-start(bf16[2,96,640]{2,1,0:T(8,128)(2,1)S(1)} %collective-permute-done.2.rest_1_), channel_id=1, source_target_pairs={{0,4},{4,8},{8,12},{12,0},{1,5},{5,9},{9,13},{13,1},{2,6},{6,10},{... | collective-permute-start | bytes 737288 | tf_op jit(solution)/shard_map/ppermute | solution.py:28
  42.9 24.3 %collective-permute-start.3 = (bf16[96,1280]{1,0:T(8,128)(2,1)S(1)}, bf16[96,1280]{1,0:T(8,128)(2,1)}, u32[]{:S(2)}, u32[]{:S(2)}) collective-permute-start(bf16[96,1280]{1,0:T(8,128)(2,1)S(1)} %collective-permute-done), channel_id=1, source_target_pairs={{0,4},{4,8},{8,12},{12,0},{1,5},{5,9},{9,13},{13,1},{2,6},{6,10},{... | collective-permute-start | bytes 737288 | tf_op jit(solution)/shard_map/ppermute | solution.py:28
  45.4 21.1 %collective-permute-start.4 = (s32[6]{0:T(128)S(1)}, s32[6]{0:T(128)S(1)}, u32[]{:S(2)}, u32[]{:S(2)}) collective-permute-start(s32[6]{0:T(128)S(1)} %collective-permute-done.1), channel_id=1, source_target_pairs={{0,4},{4,8},{8,12},{12,0},{1,5},{5,9},{9,13},{13,1},{2,6},{6,10},{... | collective-permute-start | bytes 80 | tf_op jit(solution)/shard_map/ppermute | solution.py:28
  67.3 14.2 %collective-permute-start.8 = (bf16[2,96,640]{2,1,0:T(8,128)(2,1)}, bf16[2,96,640]{2,1,0:T(8,128)(2,1)}, u32[]{:S(2)}, u32[]{:S(2)}) collective-permute-start(bf16[2,96,640]{2,1,0:T(8,128)(2,1)} %copy-done.7), channel_id=1, source_target_pairs={{0,4},{4,8},{8,12},{12,0},{1,5},{5,9},{9,13},{13,1},{2,6},{6,10},{... | collective-permute-start | bytes 737288 | tf_op jit(solution)/shard_map/ppermute | solution.py:28
  67.3 14.2 %collective-permute-start.6 = (bf16[96,1280]{1,0:T(8,128)(2,1)}, bf16[96,1280]{1,0:T(8,128)(2,1)}, u32[]{:S(2)}, u32[]{:S(2)}) collective-permute-start(bf16[96,1280]{1,0:T(8,128)(2,1)} %collective-permute-done.3), channel_id=1, source_target_pairs={{0,4},{4,8},{8,12},{12,0},{1,5},{5,9},{9,13},{13,1},{2,6},{6,10},{... | collective-permute-start | bytes 737288 | tf_op jit(solution)/shard_map/ppermute | solution.py:28
  73.4 14.8 %collective-permute-start.12 = (bf16[128,1280]{1,0:T(8,128)(2,1)}, bf16[128,1280]{1,0:T(8,128)(2,1)}, u32[]{:S(2)}, u32[]{:S(2)}) collective-permute-start(bf16[128,1280]{1,0:T(8,128)(2,1)} %dynamic-slice_convert_fusion.1), channel_id=1, source_target_pairs={{0,1},{1,0},{2,3},{3,2},{4,5},{5,4},{6,7},{7,6},{8,9},{9,8},{10,11... | collective-permute-start | bytes 983048 | tf_op jit(solution)/shard_map/ppermute | solution.py:24
  73.4 8.1 %collective-permute-start.7 = (s32[6]{0:T(128)S(1)}, s32[6]{0:T(128)S(1)}, u32[]{:S(2)}, u32[]{:S(2)}) collective-permute-start(s32[6]{0:T(128)S(1)} %collective-permute-done.4), channel_id=1, source_target_pairs={{0,4},{4,8},{8,12},{12,0},{1,5},{5,9},{9,13},{13,1},{2,6},{6,10},{... | collective-permute-start | bytes 80 | tf_op jit(solution)/shard_map/ppermute | solution.py:28
  86.4 5.3 %collective-permute-start.9 = (bf16[192,1280]{1,0:T(8,128)(2,1)}, bf16[192,1280]{1,0:T(8,128)(2,1)}, u32[]{:S(2)}, u32[]{:S(2)}) collective-permute-start(bf16[192,1280]{1,0:T(8,128)(2,1)} %dynamic-slice_convert_fusion), channel_id=1, source_target_pairs={{0,1},{1,0},{2,3},{3,2},{4,5},{5,4},{6,7},{7,6},{8,9},{9,8},{10,11... | collective-permute-start | bytes 1474568 | tf_op jit(solution)/shard_map/ppermute | solution.py:24
  86.4 51.5 %collective-permute-start.16 = (bf16[2,96,640]{2,1,0:T(8,128)(2,1)}, bf16[2,96,640]{2,1,0:T(8,128)(2,1)}, u32[]{:S(2)}, u32[]{:S(2)}) collective-permute-start(bf16[2,96,640]{2,1,0:T(8,128)(2,1)} %get-tuple-element.41.rest_0_), channel_id=1, source_target_pairs={{0,1},{1,0},{2,3},{3,2},{4,5},{5,4},{6,7},{7,6},{8,9},{9,8},{10,11... | collective-permute-start | bytes 737288 | tf_op jit(solution)/shard_map/ppermute | solution.py:24
  88.2 54.6 %collective-permute-start.15 = (bf16[4,256,640]{2,1,0:T(8,128)(2,1)}, bf16[4,256,640]{2,1,0:T(8,128)(2,1)}, u32[]{:S(2)}, u32[]{:S(2)}) collective-permute-start(bf16[4,256,640]{2,1,0:T(8,128)(2,1)} %bitcast.10.q_own), channel_id=1, source_target_pairs={{0,1},{1,0},{2,3},{3,2},{4,5},{5,4},{6,7},{7,6},{8,9},{9,8},{10,11... | collective-permute-start | bytes 3932168 | tf_op jit(solution)/shard_map/ppermute | solution.py:24
  90.2 10.8 %collective-permute-start.13 = (bf16[128,1280]{1,0:T(8,128)(2,1)}, bf16[128,1280]{1,0:T(8,128)(2,1)}, u32[]{:S(2)}, u32[]{:S(2)}) collective-permute-start(bf16[128,1280]{1,0:T(8,128)(2,1)} %fusion.9), channel_id=1, source_target_pairs={{0,2},{2,0},{1,3},{3,1},{4,6},{6,4},{5,7},{7,5},{8,10},{10,8},{9,1... | collective-permute-start | bytes 983048 | tf_op jit(solution)/shard_map/ppermute | solution.py:24
  94.0 17.2 %collective-permute-start.10 = (bf16[192,1280]{1,0:T(8,128)(2,1)}, bf16[192,1280]{1,0:T(8,128)(2,1)}, u32[]{:S(2)}, u32[]{:S(2)}) collective-permute-start(bf16[192,1280]{1,0:T(8,128)(2,1)} %fusion.8), channel_id=1, source_target_pairs={{0,2},{2,0},{1,3},{3,1},{4,6},{6,4},{5,7},{7,5},{8,10},{10,8},{9,1... | collective-permute-start | bytes 1474568 | tf_op jit(solution)/shard_map/ppermute | solution.py:24
  95.1 46.1 %collective-permute-start.17 = (bf16[2,96,640]{2,1,0:T(8,128)(2,1)}, bf16[2,96,640]{2,1,0:T(8,128)(2,1)}, u32[]{:S(2)}, u32[]{:S(2)}) collective-permute-start(bf16[2,96,640]{2,1,0:T(8,128)(2,1)} %copy-done.6), channel_id=1, source_target_pairs={{0,1},{1,0},{2,3},{3,2},{4,5},{5,4},{6,7},{7,6},{8,9},{9,8},{10,11... | collective-permute-start | bytes 737288 | tf_op jit(solution)/shard_map/ppermute | solution.py:24
  101.0 41.8 %collective-permute-start.20 = (bf16[2,640,640]{2,1,0:T(8,128)(2,1)}, bf16[2,640,640]{2,1,0:T(8,128)(2,1)}, u32[]{:S(2)}, u32[]{:S(2)}) collective-permute-start(bf16[2,640,640]{2,1,0:T(8,128)(2,1)} %all-gather.5.cloned.1.call-done.rest_8_), channel_id=1, source_target_pairs={{0,16},{16,0},{1,17},{17,1},{2,18},{18,2},{3,19},{19,3},{4,20},{20... | collective-permute-start | bytes 4915208 | tf_op jit(solution)/shard_map/ppermute | solution.py:24
  113.6 24.3 %collective-permute-start.11 = (bf16[192,1280]{1,0:T(8,128)(2,1)}, bf16[192,1280]{1,0:T(8,128)(2,1)}, u32[]{:S(2)}, u32[]{:S(2)}) collective-permute-start(bf16[192,1280]{1,0:T(8,128)(2,1)} %add_convert_fusion), channel_id=1, source_target_pairs={{0,1},{1,0},{2,3},{3,2},{4,5},{5,4},{6,7},{7,6},{8,9},{9,8},{10,11... | collective-permute-start | bytes 1474568 | tf_op jit(solution)/shard_map/ppermute | solution.py:24
  137.9 4.8 %collective-permute-start.18 = (bf16[2,96,640]{2,1,0:T(8,128)(2,1)}, bf16[2,96,640]{2,1,0:T(8,128)(2,1)S(1)}, u32[]{:S(2)}, u32[]{:S(2)}) collective-permute-start(bf16[2,96,640]{2,1,0:T(8,128)(2,1)} %copy-done.7), channel_id=1, source_target_pairs={{0,1},{1,0},{2,3},{3,2},{4,5},{5,4},{6,7},{7,6},{8,9},{9,8},{10,11... | collective-permute-start | bytes 737288 | tf_op jit(solution)/shard_map/ppermute | solution.py:24
  141.2 47.3 %collective-permute-start.22 = (bf16[2,640,640]{2,1,0:T(8,128)(2,1)}, bf16[2,640,640]{2,1,0:T(8,128)(2,1)}, u32[]{:S(2)}, u32[]{:S(2)}) collective-permute-start(bf16[2,640,640]{2,1,0:T(8,128)(2,1)} %all-gather.3.cloned.1.call-done.rest_2_), channel_id=1, source_target_pairs={{0,16},{16,0},{1,17},{17,1},{2,18},{18,2},{3,19},{19,3},{4,20},{20... | collective-permute-start | bytes 4915208 | tf_op jit(solution)/shard_map/ppermute | solution.py:24
  243.2 5.5 %collective-permute-start.26 = (f32[16,6]{1,0:T(8,128)S(1)}, f32[16,6]{1,0:T(8,128)S(1)}, u32[]{:S(2)}, u32[]{:S(2)}) collective-permute-start(f32[16,6]{1,0:T(8,128)S(1)} %get-tuple-element.43), channel_id=1, source_target_pairs={{0,4},{4,8},{8,12},{12,0},{1,5},{5,9},{9,13},{13,1},{2,6},{6,10},{... | collective-permute-start | bytes 1160 | tf_op jit(solution)/shard_map/ppermute | solution.py:311
  243.2 5.4 %collective-permute-start.27 = (f32[16,6]{1,0:T(8,128)S(1)}, f32[16,6]{1,0:T(8,128)S(1)}, u32[]{:S(2)}, u32[]{:S(2)}) collective-permute-start(f32[16,6]{1,0:T(8,128)S(1)} %get-tuple-element.45), channel_id=1, source_target_pairs={{0,8},{4,12},{8,0},{12,4},{1,9},{5,13},{9,1},{13,5},{2,10},{6,14},... | collective-permute-start | bytes 1160 | tf_op jit(solution)/shard_map/ppermute | solution.py:311
  (18 other events, 224.6 us)
Sparse Core Ops, SparseCore 0:
  9.0 57.0 all-gather.4
  73.5 39.2 all-gather.2

commit v2 on v0

--- a/solution.py
+++ b/solution.py
@@ -24,10 +24,14 @@
     return lax.ppermute(x, axis, [(0, 1), (1, 0)])
 
 
+def step_along(x, n):
+    return lax.ppermute(x, "dp", [(i, (i + 1) % n) for i in range(n)])
+
+
 def ring(x, n):
     parts = [x]
     for _ in range(n - 1):
-        parts.append(lax.ppermute(parts[-1], "dp", [(i, (i + 1) % n) for i in range(n)]))
+        parts.append(step_along(parts[-1], n))
     return parts
 
 
@@ -71,7 +75,7 @@
         in_specs=[ANY],
         out_specs=pl.BlockSpec((step, width), lambda i: (i, 0)),
         scratch_shapes=[pltpu.VMEM((2, step, width), F32), pltpu.SemaphoreType.DMA((2,))],
-        compiler_params=pltpu.CompilerParams(vmem_limit_bytes=24 * MIB),
+        compiler_params=pltpu.CompilerParams(vmem_limit_bytes=58 * MIB),
         cost_estimate=pl.CostEstimate(
             flops=4 * lam.size, bytes_accessed=8 * lam.size, transcendentals=0
         ),
@@ -79,13 +83,14 @@
     )(lam)
 
 
-def score_kernel(n, q_count, seq, first, idx, ei, qit, w, basis, q_own, q_oth, *rest):
-    xs, zs, rest = rest[:n], rest[n : 2 * n], rest[2 * n :]
+def score_kernel(n, q_count, seq, first, share, idx, ei, qit, w, q_own, q_oth, *rest):
+    e_own, e_oth, rest = rest[:n], rest[n : 2 * n], rest[2 * n :]
+    gathered, rest = rest[:-11], rest[-11:]
     out, full, tok_own, tok_oth, hid, wv, p0, p1, acc, sems, w_sem = rest
-    sub = idx[0]
+    sub, grp = idx[0], idx[1]
     chunk, all_rows, width = full.shape
     half_rows = all_rows // 2
-    q_rows, e_rows = q_own.shape[1], xs[0].shape[1]
+    q_rows, e_rows = q_own.shape[1], e_own[0].shape[1]
     j_rows = ei.shape[1]
     ex_count = ei.shape[0] // seq
     per = 128 // seq
@@ -94,12 +99,20 @@
     moves, w_moves = [], []
     for j in range(chunk):
         b = first + j
-        moves.append((basis.at[j], full.at[j]))
-        for own, oth, at, size in [(q_own, q_oth, 0, q_rows)] + [
-            (xs[k], zs[k], q_rows + k * e_rows, e_rows) for k in range(n)
-        ]:
-            moves.append((own.at[b], tok_own.at[j, pl.ds(at, size), :]))
-            moves.append((oth.at[b], tok_oth.at[j, pl.ds(at, size), :]))
+        if share:
+            piece = all_rows // n // 2
+            for half, side in zip(gathered, (grp, 1 - grp)):
+                for k in range(n):
+                    to = pl.ds(pl.multiple_of((2 * k + side) * piece, 16), piece)
+                    moves.append((half.at[j, pl.ds(k * piece, piece), :], full.at[j, to, :]))
+        else:
+            moves.append((gathered[j].at[0], full.at[j]))
+        moves.append((q_own.at[b], tok_own.at[j, pl.ds(0, q_rows), :]))
+        moves.append((q_oth.at[b], tok_oth.at[j, pl.ds(0, q_rows), :]))
+        for k in range(n):
+            to = pl.ds(q_rows + k * e_rows, e_rows)
+            moves.append((e_own[k].at[b], tok_own.at[j, to, :]))
+            moves.append((e_oth[k].at[b], tok_oth.at[j, to, :]))
         w_moves.append((w.at[pl.ds(b * j_rows, j_rows), :], wv.at[:, pl.ds(j * width, width)]))
     copies = [pltpu.make_async_copy(a, c, sems.at[i]) for i, (a, c) in enumerate(moves)]
     w_copies = [pltpu.make_async_copy(a, c, w_sem.at[i]) for i, (a, c) in enumerate(w_moves)]
@@ -116,7 +129,7 @@
     for copy in w_copies:
         copy.wait()
 
-    m_step = j_rows // 2
+    m_step = j_rows
     tiles = [(at, min(256, columns - at)) for at in range(0, columns, 256)]
 
     def outer(q, dst, at, size):
@@ -158,17 +171,21 @@
     out[...] = acc[...].sum(2)
 
 
-def chunk_scores(n, q_count, seq, first, idx, ei, qit, w, basis, q_own, q_oth, xs, zs):
-    chunk, all_rows, width = basis.shape
+def chunk_scores(n, q_count, seq, first, share, idx, ei, qit, w, q_own, q_oth, xs, zs, gathered):
+    chunk, all_rows, width = gathered[0].shape
+    if share:
+        all_rows *= 2
+    else:
+        chunk = len(gathered)
     ex_rows, j_rows = ei.shape
     q_rows = q_own.shape[1]
     ex_count = ex_rows // seq
     tokens = pltpu.VMEM((chunk, q_rows + ex_rows, width), BF)
     flops = 2 * q_count * j_rows * chunk * width * (256 + ex_rows)
     return pl.pallas_call(
-        functools.partial(score_kernel, n, q_count, seq, first),
+        functools.partial(score_kernel, n, q_count, seq, first, share),
         out_shape=jax.ShapeDtypeStruct((q_count, ex_count, 128), F32),
-        in_specs=[SMEM, VMEM, VMEM] + [ANY] * (4 + 2 * n),
+        in_specs=[SMEM, VMEM, VMEM] + [ANY] * (3 + 2 * n + len(gathered)),
         out_specs=VMEM,
         scratch_shapes=[
             pltpu.VMEM((chunk, all_rows, width), BF),
@@ -179,26 +196,31 @@
             pltpu.VMEM((j_rows, chunk * width), BF),
             pltpu.VMEM((j_rows, chunk * width), BF),
             pltpu.VMEM((q_count, ex_count, 8, 128), F32),
-            pltpu.SemaphoreType.DMA((chunk * (3 + 2 * n),)),
+            pltpu.SemaphoreType.DMA((chunk * (2 + 2 * n + 2 * n),)),
             pltpu.SemaphoreType.DMA((chunk,)),
         ],
-        compiler_params=pltpu.CompilerParams(vmem_limit_bytes=52 * MIB),
+        compiler_params=pltpu.CompilerParams(vmem_limit_bytes=58 * MIB),
         cost_estimate=pl.CostEstimate(flops=flops, bytes_accessed=12 * MIB, transcendentals=0),
         name="chunk_scores",
-    )(idx, ei, qit, w, basis, q_own, q_oth, *xs, *zs)
-
-
-def sum_features(part, sub, sizes):
+    )(idx, ei, qit, w, q_own, q_oth, *xs, *zs, *gathered)
+
+
+def sum_cores(part, sub):
     half = part.shape[0] // 2
     mine = lax.dynamic_slice_in_dim(part, sub * half, half, 0)
     other = lax.dynamic_slice_in_dim(part, (1 - sub) * half, half, 0).astype(BF)
-    mine = mine + swap(other, "sub").astype(F32)
+    return mine + swap(other, "sub").astype(F32)
+
+
+def sum_owners(mine, sizes):
     if sizes["owner"] == 2:
         total = mine + swap(mine.astype(BF), "owner").astype(F32)
     else:
         total = lax.psum(mine, "owner")
-    total = total.astype(BF)
-    rest = swap(total, "sub")
+    return total.astype(BF)
+
+
+def both_halves(total, rest, sub):
     return jnp.where(
         sub == 0, jnp.concatenate([total, rest], 0), jnp.concatenate([rest, total], 0)
     )
@@ -224,37 +246,69 @@
     j_rows = input_basis.shape[1]
     e_rows, q_rows = ex_count * seq, q_count * q_seq
     share = sizes["groups"] == 2 and rows % 32 == 0
-    idx = sub.astype(jnp.int32).reshape(1)
-
-    acts = ring(ex_acts.reshape(e_rows, input_cols), n)
+    idx = jnp.stack([sub, grp, dpi]).astype(jnp.int32)
+
+    tie = lax.optimization_barrier
+
+    chunk = 2 if blocks % 2 == 0 else 1
+    share = share and chunk < blocks
+    lead = chunk if share else 0
+    mine = hidden_basis[:lead]
+    if share:
+        mine = lax.dynamic_slice_in_dim(mine, grp * (rows // 2), rows // 2, 1)
+        mine = lax.all_gather(mine, "dp", axis=1, tiled=True)
+    later = [
+        lax.all_gather(hidden_basis[b : b + 1], "dp", axis=1, tiled=True)
+        for b in range(lead, blocks)
+    ]
+
     keep = ex_mask.astype(BF).reshape(e_rows, 1, 1)
     e_raw = jnp.transpose(ex_grads.reshape(e_rows, blocks, width) * keep, (1, 0, 2))
     q_raw = jnp.transpose(query_grads.reshape(q_rows, blocks, width), (1, 0, 2))
-    xs = ring(e_raw, n)
+
+    acts, ids = [ex_acts.reshape(e_rows, input_cols)], [ex_ids]
+    q_in = dot(query_acts.reshape(q_rows, input_cols), input_basis)
+    q_rest = None
+    for k in range(1, n):
+        act, num = step_along(acts[-1], n), step_along(ids[-1], n)
+        if k == 1:
+            act, num, q_in = tie((act, num, sum_cores(q_in, sub)))
+        elif k == 2:
+            act, num, q_in = tie((act, num, sum_owners(q_in, sizes)))
+        elif k == 3:
+            q_rest = swap(q_in, "sub")
+            act, num, q_rest, e_raw, q_raw, mine = tie((act, num, q_rest, e_raw, q_raw, mine))
+        else:
+            act, num = tie((act, num))
+        acts.append(act)
+        ids.append(num)
+    all_ids = jnp.concatenate(ids)
+    q_in = both_halves(q_in, q_rest, sub)
+    qit = jnp.transpose(q_in.reshape(q_rows // 128, 128, j_rows), (0, 2, 1))
+
+    xs, ei, ei_rest, w = [e_raw], dot(jnp.concatenate(acts, 0), input_basis), None, None
+    for k in range(1, n):
+        raw = step_along(xs[-1], n)
+        if k == 1:
+            raw, ei = tie((raw, sum_cores(ei, sub)))
+        elif k == 2:
+            raw, ei, w = tie((raw, sum_owners(ei, sizes), weights(eigenvalues)))
+        elif k == 3:
+            raw, ei_rest = tie((raw, swap(ei, "sub")))
+        xs.append(raw)
+    ei = both_halves(ei, ei_rest, sub)
+    q_oth = swap(q_raw, "sub")
     zs = [swap(x, "sub") for x in xs]
-    q_oth = swap(q_raw, "sub")
-    all_ids = jnp.concatenate(ring(ex_ids, n))
-
-    chunk = 2 if blocks % 2 == 0 else 1
-    mine = hidden_basis
-    if share:
-        mine = lax.dynamic_slice_in_dim(hidden_basis, grp * (rows // 2), rows // 2, 1)
-    full = [
-        lax.all_gather(
-            mine[b : b + chunk], ("dp", "groups") if share else "dp", axis=1, tiled=True
-        )
-        for b in range(0, blocks, chunk)
-    ]
-
-    q_in = sum_features(dot(query_acts.reshape(q_rows, input_cols), input_basis), sub, sizes)
-    qit = jnp.transpose(q_in.reshape(q_rows // 128, 128, j_rows), (0, 2, 1))
-    w = weights(eigenvalues)
-    ei = sum_features(dot(jnp.concatenate(acts, 0), input_basis), sub, sizes)
 
     total = 0.0
-    for i, basis in enumerate(full):
+    for first in range(0, blocks, chunk):
+        if first < lead:
+            gathered = [mine, swap(mine, "groups")]
+            gathered[1], later[0] = tie((gathered[1], later[0]))
+        else:
+            gathered = later[first - lead : first - lead + chunk]
         total = total + chunk_scores(
-            n, q_count, seq, i * chunk, idx, ei, qit, w, basis, q_raw, q_oth, xs, zs
+            n, q_count, seq, first, first < lead, idx, ei, qit, w, q_raw, q_oth, xs, zs, gathered
         )
     scores = total.sum(2)
 

time: 247 us -> 273 us (1.11)
  waiting for transfers between devices: 70 us -> 84.4 us
  starting transfers between devices: 23.4 us -> 32.7 us
  Pallas kernels: 99.9 us -> 107 us
  local copies, waits for them, and re-layouts: 20 us -> 16.6 us
    ppermute x9, starting transfers between devices: 13.4 us -> 23 us  [step_along(): return lax.ppermute(x, 'dp', [(i, (i + 1) % n) for i in range(n)])]
    ppermute x9, waiting for transfers between devices: 64.7 us -> 73.2 us  [step_along(): return lax.ppermute(x, 'dp', [(i, (i + 1) % n) for i in range(n)])]
    convert_element_type x4, other arithmetic: 7.85 us -> 1.75 us  [the longest x2 1.66 us: sum_owners(): return total.astype(BF)]
    unnamed x24 -> x22, local copies, waits for them, and re-layouts: 12.9 us -> 6.88 us
    pallas_call x1, Pallas kernels: 11.5 us -> 16.1 us  [weights(): pl.pallas_call(functools.partial(weight_kernel, blocks, step), grid=(bloc...]
    ppermute x11 -> x12, waiting for transfers between devices: 0.03 us -> 3.76 us  [swap(): return lax.ppermute(x, axis, [(0, 1), (1, 0)])]
    add x0 -> x2, other arithmetic: none -> 2.85 us  [sum_cores(): return mine + swap(other, 'sub').astype(F32)]
  transfers between devices with their start and end apart: 28 -> 30, of which waited for: 11 -> 13; matrix products, arithmetic and copies ran while one was open for 11% -> 10% of each run, Pallas kernels for 23% -> 22%
where the time goes in v2:
time: 273 us; the launch traced here: 272 us
  Pallas kernels  107 us (39%)
  waiting for transfers between devices  84.4 us (31%)
  starting transfers between devices  32.7 us (12%)
  local copies, waits for them, and re-layouts  16.6 us (6%)
  other arithmetic  13.4 us (5%)
  between operations  13.4 us (5%)
  matrix products  5.03 us (2%)
    pallas_call x2, Pallas kernels, chunk_scores(): pl.pallas_call(functools.partial(score_kernel, n, q_count, seq, first, sh...  90.5 us
    ppermute x9, waiting for transfers between devices, step_along(): return lax.ppermute(x, 'dp', [(i, (i + 1) % n) for i in range(n)])  73.2 us
    ppermute x9, starting transfers between devices, step_along(): return lax.ppermute(x, 'dp', [(i, (i + 1) % n) for i in range(n)])  23 us
    pallas_call x1, Pallas kernels, weights(): pl.pallas_call(functools.partial(weight_kernel, blocks, step), grid=(bloc...  16.1 us
    unnamed x22, local copies, waits for them, and re-layouts  6.88 us
  transfers between devices with their start and end apart: 30, of which 13 were waited for; matrix products, arithmetic and copies ran while one was open for 10% of the time, Pallas kernels for 22%

profile of v2, /device:TPU:0, one launch (start us, length us, event | category | flops | bytes accessed | tf_op | source)
XLA Modules:
  0.0 272.2 jit_solution(4240466610540730516)
XLA Ops:
  6.5 2.3 slice.9
  10.7 2.1 fusion.12
  15.2 2.6 collective-permute-start
  20.8 6.7 %collective-permute-done.1 = s32[6]{0:T(128)S(1)} collective-permute-done((s32[6]{0:T(128)S(1)}, s32[6]{0:T(128)S(1)}, u32[]{:S(2)}, u32[]{:S(2)}) %collective-permute-start.1) | collective-permute-done | bytes 56 | tf_op jit(solution)/shard_map/ppermute | solution.py:28
  30.8 2.9 %collective-permute-start.4 = (s32[6]{0:T(128)S(1)}, s32[6]{0:T(128)S(1)}, u32[]{:S(2)}, u32[]{:S(2)}) collective-permute-start(s32[6]{0:T(128)S(1)} %collective-permute-done.1), channel_id=1, source_target_pairs={{0,4},{4,8},{8,12},{12,0},{1,5},{5,9},{9,13},{13,1},{2,6},{6,10},{... | collective-permute-start | bytes 80 | tf_op jit(solution)/shard_map/ppermute | solution.py:28
  33.7 3.1 %collective-permute-done.5 = bf16[128,1280]{1,0:T(8,128)(2,1)S(1)} collective-permute-done((bf16[128,1280]{1,0:T(8,128)(2,1)S(1)}, bf16[128,1280]{1,0:T(8,128)(2,1)S(1)}, u32[]{:S(2)}, u32[]{:S(2)}) %collective-permute-start.5) | collective-permute-done | bytes 327712 | tf_op jit(solution)/shard_map/ppermute | solution.py:24
  37.6 8.2 %collective-permute-done.4 = s32[6]{0:T(128)S(1)} collective-permute-done((s32[6]{0:T(128)S(1)}, s32[6]{0:T(128)S(1)}, u32[]{:S(2)}, u32[]{:S(2)}) %collective-permute-start.4) | collective-permute-done | bytes 56 | tf_op jit(solution)/shard_map/ppermute | solution.py:28
  48.9 2.6 copy.14
  51.5 4.1 %collective-permute-start.6 = (bf16[96,1280]{1,0:T(8,128)(2,1)}, bf16[96,1280]{1,0:T(8,128)(2,1)}, u32[]{:S(2)}, u32[]{:S(2)}) collective-permute-start(bf16[96,1280]{1,0:T(8,128)(2,1)} %copy-done.9), channel_id=1, source_target_pairs={{0,4},{4,8},{8,12},{12,0},{1,5},{5,9},{9,13},{13,1},{2,6},{6,10},{... | collective-permute-start | bytes 737288 | tf_op jit(solution)/shard_map/ppermute | solution.py:28
  57.5 2.8 %collective-permute-start.7 = (s32[6]{0:T(128)S(1)}, s32[6]{0:T(128)S(1)}, u32[]{:S(2)}, u32[]{:S(2)}) collective-permute-start(s32[6]{0:T(128)S(1)} %collective-permute-done.4), channel_id=1, source_target_pairs={{0,4},{4,8},{8,12},{12,0},{1,5},{5,9},{9,13},{13,1},{2,6},{6,10},{... | collective-permute-start | bytes 80 | tf_op jit(solution)/shard_map/ppermute | solution.py:28
  60.3 5.7 %collective-permute-done.7 = s32[6]{0:T(128)S(1)} collective-permute-done((s32[6]{0:T(128)S(1)}, s32[6]{0:T(128)S(1)}, u32[]{:S(2)}, u32[]{:S(2)}) %collective-permute-start.7) | collective-permute-done | bytes 56 | tf_op jit(solution)/shard_map/ppermute | solution.py:28
  66.0 2.7 fusion
  74.6 22.8 %collective-permute-done.9.rest_1_ = bf16[4,96,640]{2,1,0:T(8,128)(2,1)S(1)} collective-permute-done((bf16[4,96,640]{2,1,0:T(8,128)(2,1)}, bf16[4,96,640]{2,1,0:T(8,128)(2,1)S(1)}, u32[]{:S(2)}, u32[]{:S(2)}) %collective-permute-start.9) | collective-permute-done | bytes 491552 | tf_op jit(solution)/shard_map/ppermute | solution.py:28
  97.6 16.1 %weights.1.w = f32[5120,640]{1,0:T(8,128)} custom-call(f32[1280,4,640]{2,1,0:T(4,128)} %lam.1), custom_call_target="tpu_custom_call" | custom-call | flops 13107200 | bytes 26214400 | tf_op jit(solution)/shard_map/weights/pallas_call | solution.py:71
  113.9 7.6 %collective-permute-start.11 = (bf16[4,96,640]{2,1,0:T(8,128)(2,1)S(1)}, bf16[4,96,640]{2,1,0:T(8,128)(2,1)}, u32[]{:S(2)}, u32[]{:S(2)}) collective-permute-start(bf16[4,96,640]{2,1,0:T(8,128)(2,1)S(1)} %collective-permute-done.9.rest_1_), channel_id=1, source_target_pairs={{0,4},{4,8},{8,12},{12,0},{1,5},{5,9},{9,13},{13,1},{2,6},{6,10},{... | collective-permute-start | bytes 1474568 | tf_op jit(solution)/shard_map/ppermute | solution.py:28
  122.4 14.1 %collective-permute-done.11.rest_2_ = bf16[4,96,640]{2,1,0:T(8,128)(2,1)} collective-permute-done((bf16[4,96,640]{2,1,0:T(8,128)(2,1)S(1)}, bf16[4,96,640]{2,1,0:T(8,128)(2,1)}, u32[]{:S(2)}, u32[]{:S(2)}) %collective-permute-start.11) | collective-permute-done | bytes 491552 | tf_op jit(solution)/shard_map/ppermute | solution.py:28
  137.6 15.6 %collective-permute-done.13.rest_3_ = bf16[4,96,640]{2,1,0:T(8,128)(2,1)} collective-permute-done((bf16[4,96,640]{2,1,0:T(8,128)(2,1)}, bf16[4,96,640]{2,1,0:T(8,128)(2,1)}, u32[]{:S(2)}, u32[]{:S(2)}) %collective-permute-start.13) | collective-permute-done | bytes 491552 | tf_op jit(solution)/shard_map/ppermute | solution.py:28
  153.9 2.3 maximum_select_fusion.1
  156.2 2.2 copy.15
  158.4 2.7 maximum_select_fusion.ei
  161.2 44.8 %chunk_scores.2 = f32[16,24,128]{2,1,0:T(8,128)} custom-call(s32[3]{0:T(128)} %pad_add_fusion.idx, bf16[384,1280]{1,0:T(8,128)(2,1)} %maximum_select_fusion.ei, bf16[2,1280,128]{2,1,0:T(8,128)(2,1)} %bitcast.18, f32[5120,640]{1,0:T(8,128)} %weights.1.w, bf16[4,256,640]{2,1,0:T(8,128)(2,1)} %bitcast.8.q_own, ...), custom_call_target="tpu_custom_call" | custom-call | flops 33554432000 | bytes 12582912 | tf_op jit(solution)/shard_map/chunk_scores/pallas_call | solution.py:185
  206.1 45.7 %chunk_scores.3 = f32[16,24,128]{2,1,0:T(8,128)} custom-call(s32[3]{0:T(128)} %pad_add_fusion.idx, bf16[384,1280]{1,0:T(8,128)(2,1)} %maximum_select_fusion.ei, bf16[2,1280,128]{2,1,0:T(8,128)(2,1)} %bitcast.19, f32[5120,640]{1,0:T(8,128)} %weights.1.w, bf16[4,256,640]{2,1,0:T(8,128)(2,1)} %bitcast.8.q_own, ...), custom_call_target="tpu_custom_call" | custom-call | flops 33554432000 | bytes 12582912 | tf_op jit(solution)/shard_map/chunk_scores/pallas_call | solution.py:185
  253.0 2.0 collective-permute-start.23
  256.4 2.4 collective-permute-done.22
  (91 shorter events, 34.6 us)
Async XLA Ops:
  6.5 59.5 %all-gather.4.cloned.1.call-start = ((), (), s32[]{:S(2)}) async-start(), calls=%async_computation | async-start | bytes 2048000 | tf_op jit(solution)/shard_map/all_gather | solution.py:259
  10.7 150.5 %all-gather.6.cloned.1.call-start = ((), (), s32[]{:S(2)}) async-start(), calls=%async_computation.1 | async-start | bytes 2048000 | tf_op jit(solution)/shard_map/all_gather | solution.py:261
  14.8 4.6 %collective-permute-start.2 = (bf16[128,1280]{1,0:T(8,128)(2,1)}, bf16[128,1280]{1,0:T(8,128)(2,1)}, u32[]{:S(2)}, u32[]{:S(2)}) collective-permute-start(bf16[128,1280]{1,0:T(8,128)(2,1)} %dynamic-slice_convert_fusion.1), channel_id=1, source_target_pairs={{0,1},{1,0},{2,3},{3,2},{4,5},{5,4},{6,7},{7,6},{8,9},{9,8},{10,11... | collective-permute-start | bytes 983048 | tf_op jit(solution)/shard_map/ppermute | solution.py:24
  15.2 12.3 %collective-permute-start = (bf16[96,1280]{1,0:T(8,128)(2,1)S(1)}, bf16[96,1280]{1,0:T(8,128)(2,1)}, u32[]{:S(2)}, u32[]{:S(2)}) collective-permute-start(bf16[96,1280]{1,0:T(8,128)(2,1)S(1)} %bitcast.25), channel_id=1, source_target_pairs={{0,4},{4,8},{8,12},{12,0},{1,5},{5,9},{9,13},{13,1},{2,6},{6,10},{... | collective-permute-start | bytes 737288 | tf_op jit(solution)/shard_map/ppermute | solution.py:28
  17.8 9.7 %collective-permute-start.1 = (s32[6]{0:T(128)S(1)}, s32[6]{0:T(128)S(1)}, u32[]{:S(2)}, u32[]{:S(2)}) collective-permute-start(s32[6]{0:T(128)S(1)} %copy-done.6), channel_id=1, source_target_pairs={{0,4},{4,8},{8,12},{12,0},{1,5},{5,9},{9,13},{13,1},{2,6},{6,10},{... | collective-permute-start | bytes 80 | tf_op jit(solution)/shard_map/ppermute | solution.py:28
  27.6 9.2 %collective-permute-start.5 = (bf16[128,1280]{1,0:T(8,128)(2,1)S(1)}, bf16[128,1280]{1,0:T(8,128)(2,1)S(1)}, u32[]{:S(2)}, u32[]{:S(2)}) collective-permute-start(bf16[128,1280]{1,0:T(8,128)(2,1)S(1)} %convert_element_type.36), channel_id=1, source_target_pairs={{0,2},{2,0},{1,3},{3,1},{4,6},{6,4},{5,7},{7,5},{8,10},{10,8},{9,1... | collective-permute-start | bytes 983048 | tf_op jit(solution)/shard_map/ppermute | solution.py:24
  29.3 16.5 %collective-permute-start.3 = (bf16[96,1280]{1,0:T(8,128)(2,1)}, bf16[96,1280]{1,0:T(8,128)(2,1)S(1)}, u32[]{:S(2)}, u32[]{:S(2)}) collective-permute-start(bf16[96,1280]{1,0:T(8,128)(2,1)} %collective-permute-done), channel_id=1, source_target_pairs={{0,4},{4,8},{8,12},{12,0},{1,5},{5,9},{9,13},{13,1},{2,6},{6,10},{... | collective-permute-start | bytes 737288 | tf_op jit(solution)/shard_map/ppermute | solution.py:28
  30.8 15.0 %collective-permute-start.4 = (s32[6]{0:T(128)S(1)}, s32[6]{0:T(128)S(1)}, u32[]{:S(2)}, u32[]{:S(2)}) collective-permute-start(s32[6]{0:T(128)S(1)} %collective-permute-done.1), channel_id=1, source_target_pairs={{0,4},{4,8},{8,12},{12,0},{1,5},{5,9},{9,13},{13,1},{2,6},{6,10},{... | collective-permute-start | bytes 80 | tf_op jit(solution)/shard_map/ppermute | solution.py:28
  45.8 20.2 %collective-permute-start.8 = (bf16[128,1280]{1,0:T(8,128)(2,1)}, bf16[128,1280]{1,0:T(8,128)(2,1)}, u32[]{:S(2)}, u32[]{:S(2)}) collective-permute-start(bf16[128,1280]{1,0:T(8,128)(2,1)} %add_convert_fusion.1), channel_id=1, source_target_pairs={{0,1},{1,0},{2,3},{3,2},{4,5},{5,4},{6,7},{7,6},{8,9},{9,8},{10,11... | collective-permute-start | bytes 983048 | tf_op jit(solution)/shard_map/ppermute | solution.py:24
  46.9 159.2 %all-gather.8.cloned.1.call-start = ((), (), s32[]{:S(2)}) async-start(), calls=%async_computation.2 | async-start | bytes 2048000 | tf_op jit(solution)/shard_map/all_gather | solution.py:261
  51.5 14.6 %collective-permute-start.6 = (bf16[96,1280]{1,0:T(8,128)(2,1)}, bf16[96,1280]{1,0:T(8,128)(2,1)}, u32[]{:S(2)}, u32[]{:S(2)}) collective-permute-start(bf16[96,1280]{1,0:T(8,128)(2,1)} %copy-done.9), channel_id=1, source_target_pairs={{0,4},{4,8},{8,12},{12,0},{1,5},{5,9},{9,13},{13,1},{2,6},{6,10},{... | collective-permute-start | bytes 737288 | tf_op jit(solution)/shard_map/ppermute | solution.py:28
  57.5 8.5 %collective-permute-start.7 = (s32[6]{0:T(128)S(1)}, s32[6]{0:T(128)S(1)}, u32[]{:S(2)}, u32[]{:S(2)}) collective-permute-start(s32[6]{0:T(128)S(1)} %collective-permute-done.4), channel_id=1, source_target_pairs={{0,4},{4,8},{8,12},{12,0},{1,5},{5,9},{9,13},{13,1},{2,6},{6,10},{... | collective-permute-start | bytes 80 | tf_op jit(solution)/shard_map/ppermute | solution.py:28
  70.9 26.5 %collective-permute-start.9 = (bf16[4,96,640]{2,1,0:T(8,128)(2,1)}, bf16[4,96,640]{2,1,0:T(8,128)(2,1)S(1)}, u32[]{:S(2)}, u32[]{:S(2)}) collective-permute-start(bf16[4,96,640]{2,1,0:T(8,128)(2,1)} %bitcast.20), channel_id=1, source_target_pairs={{0,4},{4,8},{8,12},{12,0},{1,5},{5,9},{9,13},{13,1},{2,6},{6,10},{... | collective-permute-start | bytes 1474568 | tf_op jit(solution)/shard_map/ppermute | solution.py:28
  70.9 82.9 %collective-permute-start.20 = (bf16[2,640,640]{2,1,0:T(8,128)(2,1)}, bf16[2,640,640]{2,1,0:T(8,128)(2,1)}, u32[]{:S(2)}, u32[]{:S(2)}) collective-permute-start(bf16[2,640,640]{2,1,0:T(8,128)(2,1)} %all-gather.4.cloned.1.call-done.rest_8_), channel_id=1, source_target_pairs={{0,16},{16,0},{1,17},{17,1},{2,18},{18,2},{3,19},{19,3},{4,20},{20... | collective-permute-start | bytes 4915208 | tf_op jit(solution)/shard_map/ppermute | solution.py:24
  97.4 24.1 %collective-permute-start.12 = (bf16[192,1280]{1,0:T(8,128)(2,1)S(1)}, bf16[192,1280]{1,0:T(8,128)(2,1)S(1)}, u32[]{:S(2)}, u32[]{:S(2)}) collective-permute-start(bf16[192,1280]{1,0:T(8,128)(2,1)S(1)} %convert_element_type.42), channel_id=1, source_target_pairs={{0,2},{2,0},{1,3},{3,1},{4,6},{6,4},{5,7},{7,5},{8,10},{10,8},{9,1... | collective-permute-start | bytes 1474568 | tf_op jit(solution)/shard_map/ppermute | solution.py:24
  113.8 47.4 %collective-permute-start.15 = (bf16[4,256,640]{2,1,0:T(8,128)(2,1)}, bf16[4,256,640]{2,1,0:T(8,128)(2,1)}, u32[]{:S(2)}, u32[]{:S(2)}) collective-permute-start(bf16[4,256,640]{2,1,0:T(8,128)(2,1)} %bitcast.8.q_own), channel_id=1, source_target_pairs={{0,1},{1,0},{2,3},{3,2},{4,5},{5,4},{6,7},{7,6},{8,9},{9,8},{10,11... | collective-permute-start | bytes 3932168 | tf_op jit(solution)/shard_map/ppermute | solution.py:24
  113.9 22.6 %collective-permute-start.11 = (bf16[4,96,640]{2,1,0:T(8,128)(2,1)S(1)}, bf16[4,96,640]{2,1,0:T(8,128)(2,1)}, u32[]{:S(2)}, u32[]{:S(2)}) collective-permute-start(bf16[4,96,640]{2,1,0:T(8,128)(2,1)S(1)} %collective-permute-done.9.rest_1_), channel_id=1, source_target_pairs={{0,4},{4,8},{8,12},{12,0},{1,5},{5,9},{9,13},{13,1},{2,6},{6,10},{... | collective-permute-start | bytes 1474568 | tf_op jit(solution)/shard_map/ppermute | solution.py:28
  136.5 16.8 %collective-permute-start.13 = (bf16[4,96,640]{2,1,0:T(8,128)(2,1)}, bf16[4,96,640]{2,1,0:T(8,128)(2,1)}, u32[]{:S(2)}, u32[]{:S(2)}) collective-permute-start(bf16[4,96,640]{2,1,0:T(8,128)(2,1)} %collective-permute-done.11.rest_2_), channel_id=1, source_target_pairs={{0,4},{4,8},{8,12},{12,0},{1,5},{5,9},{9,13},{13,1},{2,6},{6,10},{... | collective-permute-start | bytes 1474568 | tf_op jit(solution)/shard_map/ppermute | solution.py:28
  136.5 16.8 %collective-permute-start.14 = (bf16[192,1280]{1,0:T(8,128)(2,1)}, bf16[192,1280]{1,0:T(8,128)(2,1)}, u32[]{:S(2)}, u32[]{:S(2)}) collective-permute-start(bf16[192,1280]{1,0:T(8,128)(2,1)} %add_convert_fusion), channel_id=1, source_target_pairs={{0,1},{1,0},{2,3},{3,2},{4,5},{5,4},{6,7},{7,6},{8,9},{9,8},{10,11... | collective-permute-start | bytes 1474568 | tf_op jit(solution)/shard_map/ppermute | solution.py:24
  137.1 24.0 %collective-permute-start.16 = (bf16[4,96,640]{2,1,0:T(8,128)(2,1)}, bf16[4,96,640]{2,1,0:T(8,128)(2,1)}, u32[]{:S(2)}, u32[]{:S(2)}) collective-permute-start(bf16[4,96,640]{2,1,0:T(8,128)(2,1)} %bitcast.21), channel_id=1, source_target_pairs={{0,1},{1,0},{2,3},{3,2},{4,5},{5,4},{6,7},{7,6},{8,9},{9,8},{10,11... | collective-permute-start | bytes 1474568 | tf_op jit(solution)/shard_map/ppermute | solution.py:24
  153.3 7.9 %collective-permute-start.17 = (bf16[4,96,640]{2,1,0:T(8,128)(2,1)}, bf16[4,96,640]{2,1,0:T(8,128)(2,1)}, u32[]{:S(2)}, u32[]{:S(2)}) collective-permute-start(bf16[4,96,640]{2,1,0:T(8,128)(2,1)} %copy-done.7), channel_id=1, source_target_pairs={{0,1},{1,0},{2,3},{3,2},{4,5},{5,4},{6,7},{7,6},{8,9},{9,8},{10,11... | collective-permute-start | bytes 1474568 | tf_op jit(solution)/shard_map/ppermute | solution.py:24
  153.3 7.9 %collective-permute-start.18 = (bf16[4,96,640]{2,1,0:T(8,128)(2,1)}, bf16[4,96,640]{2,1,0:T(8,128)(2,1)}, u32[]{:S(2)}, u32[]{:S(2)}) collective-permute-start(bf16[4,96,640]{2,1,0:T(8,128)(2,1)} %collective-permute-done.11.rest_2_), channel_id=1, source_target_pairs={{0,1},{1,0},{2,3},{3,2},{4,5},{5,4},{6,7},{7,6},{8,9},{9,8},{10,11... | collective-permute-start | bytes 1474568 | tf_op jit(solution)/shard_map/ppermute | solution.py:24
  153.8 7.4 %collective-permute-start.19 = (bf16[4,96,640]{2,1,0:T(8,128)(2,1)}, bf16[4,96,640]{2,1,0:T(8,128)(2,1)}, u32[]{:S(2)}, u32[]{:S(2)}) collective-permute-start(bf16[4,96,640]{2,1,0:T(8,128)(2,1)} %collective-permute-done.13.rest_3_), channel_id=1, source_target_pairs={{0,1},{1,0},{2,3},{3,2},{4,5},{5,4},{6,7},{7,6},{8,9},{9,8},{10,11... | collective-permute-start | bytes 1474568 | tf_op jit(solution)/shard_map/ppermute | solution.py:24
  258.9 6.0 %collective-permute-start.24 = (f32[16,6]{1,0:T(8,128)S(1)}, f32[16,6]{1,0:T(8,128)S(1)}, u32[]{:S(2)}, u32[]{:S(2)}) collective-permute-start(f32[16,6]{1,0:T(8,128)S(1)} %get-tuple-element.49), channel_id=1, source_target_pairs={{0,4},{4,8},{8,12},{12,0},{1,5},{5,9},{9,13},{13,1},{2,6},{6,10},{... | collective-permute-start | bytes 1160 | tf_op jit(solution)/shard_map/ppermute | solution.py:330
  (16 other events, 147.9 us)
Sparse Core Ops, SparseCore 0:
  10.8 47.9 all-gather.3
  60.4 47.7 all-gather.5
  136.6 41.9 all-gather.7

commit v3 on v0

--- a/solution.py
+++ b/solution.py
@@ -24,10 +24,14 @@
     return lax.ppermute(x, axis, [(0, 1), (1, 0)])
 
 
+def step_along(x, n):
+    return lax.ppermute(x, "dp", [(i, (i + 1) % n) for i in range(n)])
+
+
 def ring(x, n):
     parts = [x]
     for _ in range(n - 1):
-        parts.append(lax.ppermute(parts[-1], "dp", [(i, (i + 1) % n) for i in range(n)]))
+        parts.append(step_along(parts[-1], n))
     return parts
 
 
@@ -71,7 +75,7 @@
         in_specs=[ANY],
         out_specs=pl.BlockSpec((step, width), lambda i: (i, 0)),
         scratch_shapes=[pltpu.VMEM((2, step, width), F32), pltpu.SemaphoreType.DMA((2,))],
-        compiler_params=pltpu.CompilerParams(vmem_limit_bytes=24 * MIB),
+        compiler_params=pltpu.CompilerParams(vmem_limit_bytes=58 * MIB),
         cost_estimate=pl.CostEstimate(
             flops=4 * lam.size, bytes_accessed=8 * lam.size, transcendentals=0
         ),
@@ -182,7 +186,7 @@
             pltpu.SemaphoreType.DMA((chunk * (3 + 2 * n),)),
             pltpu.SemaphoreType.DMA((chunk,)),
         ],
-        compiler_params=pltpu.CompilerParams(vmem_limit_bytes=52 * MIB),
+        compiler_params=pltpu.CompilerParams(vmem_limit_bytes=58 * MIB),
         cost_estimate=pl.CostEstimate(flops=flops, bytes_accessed=12 * MIB, transcendentals=0),
         name="chunk_scores",
     )(idx, ei, qit, w, basis, q_own, q_oth, *xs, *zs)
@@ -226,29 +230,38 @@
     share = sizes["groups"] == 2 and rows % 32 == 0
     idx = sub.astype(jnp.int32).reshape(1)
 
-    acts = ring(ex_acts.reshape(e_rows, input_cols), n)
+    chunk = 2 if blocks % 2 == 0 else 1
+    mine = hidden_basis
+    if share:
+        mine = lax.dynamic_slice_in_dim(hidden_basis, grp * (rows // 2), rows // 2, 1)
+    mine = [mine[b : b + chunk] for b in range(0, blocks, chunk)]
+    acts, *mine = lax.optimization_barrier((ex_acts.reshape(e_rows, input_cols), *mine))
+    full = [
+        lax.all_gather(part, ("dp", "groups") if share else "dp", axis=1, tiled=True)
+        for part in mine
+    ]
+
+    w = weights(eigenvalues)
+    acts, ids = [acts], [ex_ids]
+    for k in range(1, n):
+        last = step_along(acts[-1], n), step_along(ids[-1], n)
+        if k == 2:
+            *last, w = lax.optimization_barrier((*last, w))
+        else:
+            last = lax.optimization_barrier(last)
+        acts.append(last[0])
+        ids.append(last[1])
+    all_ids = jnp.concatenate(ids)
+
     keep = ex_mask.astype(BF).reshape(e_rows, 1, 1)
     e_raw = jnp.transpose(ex_grads.reshape(e_rows, blocks, width) * keep, (1, 0, 2))
     q_raw = jnp.transpose(query_grads.reshape(q_rows, blocks, width), (1, 0, 2))
     xs = ring(e_raw, n)
     zs = [swap(x, "sub") for x in xs]
     q_oth = swap(q_raw, "sub")
-    all_ids = jnp.concatenate(ring(ex_ids, n))
-
-    chunk = 2 if blocks % 2 == 0 else 1
-    mine = hidden_basis
-    if share:
-        mine = lax.dynamic_slice_in_dim(hidden_basis, grp * (rows // 2), rows // 2, 1)
-    full = [
-        lax.all_gather(
-            mine[b : b + chunk], ("dp", "groups") if share else "dp", axis=1, tiled=True
-        )
-        for b in range(0, blocks, chunk)
-    ]
 
     q_in = sum_features(dot(query_acts.reshape(q_rows, input_cols), input_basis), sub, sizes)
     qit = jnp.transpose(q_in.reshape(q_rows // 128, 128, j_rows), (0, 2, 1))
-    w = weights(eigenvalues)
     ei = sum_features(dot(jnp.concatenate(acts, 0), input_basis), sub, sizes)
 
     total = 0.0

time: 247 us -> 249 us (level)
  local copies, waits for them, and re-layouts: 20 us -> 10.6 us
  Pallas kernels: 99.9 us -> 107 us
  starting transfers between devices: 23.4 us -> 26.1 us
  waiting for transfers between devices: 70 us -> 72.6 us
    unnamed x24, local copies, waits for them, and re-layouts: 12.9 us -> 3.5 us
    pallas_call x1, Pallas kernels: 11.5 us -> 16.1 us  [weights(): pl.pallas_call(functools.partial(weight_kernel, blocks, step), grid=(bloc...]
    ppermute x9, starting transfers between devices: 13.4 us -> 16.6 us  [step_along(): return lax.ppermute(x, 'dp', [(i, (i + 1) % n) for i in range(n)])]
  transfers between devices with their start and end apart: 28 -> 28, of which waited for: 11 -> 11; matrix products, arithmetic and copies ran while one was open for 11% -> 10% of each run, Pallas kernels for 23% -> 25%
where the time goes in v3:
time: 249 us; the launch traced here: 248 us
  Pallas kernels  107 us (43%)
  waiting for transfers between devices  72.6 us (29%)
  starting transfers between devices  26.1 us (10%)
  other arithmetic  15 us (6%)
  between operations  13.6 us (5%)
  local copies, waits for them, and re-layouts  10.6 us (4%)
  matrix products  3.83 us (2%)
    pallas_call x2, Pallas kernels, chunk_scores(): pl.pallas_call(functools.partial(score_kernel, n, q_count, seq, first), o...  90.4 us
    ppermute x9, waiting for transfers between devices, step_along(): return lax.ppermute(x, 'dp', [(i, (i + 1) % n) for i in range(n)])  65.3 us
    ppermute x9, starting transfers between devices, step_along(): return lax.ppermute(x, 'dp', [(i, (i + 1) % n) for i in range(n)])  16.6 us
    pallas_call x1, Pallas kernels, weights(): pl.pallas_call(functools.partial(weight_kernel, blocks, step), grid=(bloc...  16.1 us
    select_n x2, other arithmetic, sum_features(): jnp.where(sub == 0, jnp.concatenate([total, rest], 0), jnp.concatenate([r...  4.98 us
  transfers between devices with their start and end apart: 28, of which 11 were waited for; matrix products, arithmetic and copies ran while one was open for 10% of the time, Pallas kernels for 25%

profile of v3, /device:TPU:0, one launch (start us, length us, event | category | flops | bytes accessed | tf_op | source)
XLA Modules:
  0.0 248.4 jit_solution(3014868650982807858)
XLA Ops:
  6.6 2.3 constant_dynamic-slice_fusion.4
  8.9 3.1 %collective-permute-start = (bf16[96,1280]{1,0:T(8,128)(2,1)S(1)}, bf16[96,1280]{1,0:T(8,128)(2,1)}, u32[]{:S(2)}, u32[]{:S(2)}) collective-permute-start(bf16[96,1280]{1,0:T(8,128)(2,1)S(1)} %bitcast.19), channel_id=1, source_target_pairs={{0,4},{4,8},{8,12},{12,0},{1,5},{5,9},{9,13},{13,1},{2,6},{6,10},{... | collective-permute-start | bytes 737288 | tf_op jit(solution)/shard_map/ppermute | solution.py:28
  13.6 6.5 %collective-permute-done.1 = s32[6]{0:T(128)S(1)} collective-permute-done((s32[6]{0:T(128)S(1)}, s32[6]{0:T(128)S(1)}, u32[]{:S(2)}, u32[]{:S(2)}) %collective-permute-start.1) | collective-permute-done | bytes 56 | tf_op jit(solution)/shard_map/ppermute | solution.py:28
  20.1 1.9 copy.15
  22.1 16.1 %weights.1.w = f32[5120,640]{1,0:T(8,128)} custom-call(f32[1280,4,640]{2,1,0:T(4,128)} %lam.1), custom_call_target="tpu_custom_call" | custom-call | flops 13107200 | bytes 26214400 | tf_op jit(solution)/shard_map/weights/pallas_call | solution.py:71
  39.6 4.0 %collective-permute-done.3 = s32[6]{0:T(128)S(1)} collective-permute-done((s32[6]{0:T(128)S(1)}, s32[6]{0:T(128)S(1)}, u32[]{:S(2)}, u32[]{:S(2)}) %collective-permute-start.3) | collective-permute-done | bytes 56 | tf_op jit(solution)/shard_map/ppermute | solution.py:28
  45.6 2.1 collective-permute-start.5
  47.7 29.7 %collective-permute-done.5 = s32[6]{0:T(128)S(1)} collective-permute-done((s32[6]{0:T(128)S(1)}, s32[6]{0:T(128)S(1)}, u32[]{:S(2)}, u32[]{:S(2)}) %collective-permute-start.5) | collective-permute-done | bytes 56 | tf_op jit(solution)/shard_map/ppermute | solution.py:28
  77.5 2.6 %fusion = f32[384,1280]{1,0:T(8,128)S(1)} fusion(bf16[1280,1280]{1,0:T(8,128)(2,1)S(1)} %copy-done, bf16[96,1280]{1,0:T(8,128)(2,1)} %collective-permute-done.4, bf16[96,1280]{1,0:T(8,128)(2,1)} %collective-permute-done.2, bf16[96,1280]{1,0:T(8,128)(2,1)} %collective-permute-done, bf16[96,1280]{1,0:T(8,128)(2,1)S(1)} %bitcast.20), kind=kOutput, calls=%fused_computation | convolution fusion | flops 1262223360 | bytes 6225920 | tf_op jit(solution)/shard_map/dot_general | solution.py:20
  83.8 6.7 %collective-permute-start.14 = (bf16[4,96,640]{2,1,0:T(8,128)(2,1)}, bf16[4,96,640]{2,1,0:T(8,128)(2,1)}, u32[]{:S(2)}, u32[]{:S(2)}) collective-permute-start(bf16[4,96,640]{2,1,0:T(8,128)(2,1)} %collective-permute-done.13.rest_1_), channel_id=1, source_target_pairs={{0,4},{4,8},{8,12},{12,0},{1,5},{5,9},{9,13},{13,1},{2,6},{6,10},{... | collective-permute-start | bytes 1474568 | tf_op jit(solution)/shard_map/ppermute | solution.py:28
  90.6 2.3 fusion.8
  97.5 11.2 %collective-permute-done.14.rest_2_ = bf16[4,96,640]{2,1,0:T(8,128)(2,1)} collective-permute-done((bf16[4,96,640]{2,1,0:T(8,128)(2,1)}, bf16[4,96,640]{2,1,0:T(8,128)(2,1)}, u32[]{:S(2)}, u32[]{:S(2)}) %collective-permute-start.14) | collective-permute-done | bytes 491552 | tf_op jit(solution)/shard_map/ppermute | solution.py:28
  109.4 2.5 add_convert_fusion
  112.9 1.8 add_convert_fusion.1
  116.8 13.8 %collective-permute-done.15.rest_3_ = bf16[4,96,640]{2,1,0:T(8,128)(2,1)} collective-permute-done((bf16[4,96,640]{2,1,0:T(8,128)(2,1)}, bf16[4,96,640]{2,1,0:T(8,128)(2,1)}, u32[]{:S(2)}, u32[]{:S(2)}) %collective-permute-start.15) | collective-permute-done | bytes 491552 | tf_op jit(solution)/shard_map/ppermute | solution.py:28
  131.2 2.3 maximum_select_fusion.1
  133.4 2.2 copy.13
  135.6 2.7 %maximum_select_fusion.ei = bf16[384,1280]{1,0:T(8,128)(2,1)} fusion(bf16[192,1280]{1,0:T(8,128)(2,1)} %collective-permute-done.8, bf16[192,1280]{1,0:T(8,128)(2,1)} %add_convert_fusion, pred[]{:T(512)S(6)} %eq.8), kind=kLoop, calls=%fused_computation.8 | loop fusion | flops 4423680 | bytes 1966081 | tf_op jit(solution)/shard_map/jit(_where)/select_n | solution.py:206
  138.4 45.2 %chunk_scores.3 = f32[16,24,128]{2,1,0:T(8,128)} custom-call(s32[1]{0:T(128)} %bitcast.idx, bf16[384,1280]{1,0:T(8,128)(2,1)} %maximum_select_fusion.ei, bf16[2,1280,128]{2,1,0:T(8,128)(2,1)} %bitcast.16, f32[5120,640]{1,0:T(8,128)} %weights.1.w, bf16[2,1280,640]{2,1,0:T(8,128)(2,1)} %all-gather.5.cloned.1.call-done.basis, ...), custom_call_target="tpu_custom_call" | custom-call | flops 33554432000 | bytes 12582912 | tf_op jit(solution)/shard_map/chunk_scores/pallas_call | solution.py:172
  183.6 45.3 %chunk_scores.2 = f32[16,24,128]{2,1,0:T(8,128)} custom-call(s32[1]{0:T(128)} %bitcast.idx, bf16[384,1280]{1,0:T(8,128)(2,1)} %maximum_select_fusion.ei, bf16[2,1280,128]{2,1,0:T(8,128)(2,1)} %bitcast.17, f32[5120,640]{1,0:T(8,128)} %weights.1.w, bf16[2,1280,640]{2,1,0:T(8,128)(2,1)} %all-gather.3.cloned.1.call-done.basis, ...), custom_call_target="tpu_custom_call" | custom-call | flops 33554432000 | bytes 12582912 | tf_op jit(solution)/shard_map/chunk_scores/pallas_call | solution.py:172
  232.0 1.8 collective-permute-done.21
  234.8 2.1 collective-permute-start.24
  236.9 1.7 collective-permute-start.25
  238.6 1.6 collective-permute-done.23
  (83 shorter events, 23.3 us)
Async XLA Ops:
  6.5 131.8 %all-gather.5.cloned.1.call-start = ((), (), s32[]{:S(2)}) async-start(), calls=%async_computation.1 | async-start | bytes 3686400 | tf_op jit(solution)/shard_map/all_gather | solution.py:240
  8.9 174.7 %all-gather.3.cloned.1.call-start = ((), (), s32[]{:S(2)}) async-start(), calls=%async_computation | async-start | bytes 3686400 | tf_op jit(solution)/shard_map/all_gather | solution.py:240
  8.9 11.2 %collective-permute-start = (bf16[96,1280]{1,0:T(8,128)(2,1)S(1)}, bf16[96,1280]{1,0:T(8,128)(2,1)}, u32[]{:S(2)}, u32[]{:S(2)}) collective-permute-start(bf16[96,1280]{1,0:T(8,128)(2,1)S(1)} %bitcast.19), channel_id=1, source_target_pairs={{0,4},{4,8},{8,12},{12,0},{1,5},{5,9},{9,13},{13,1},{2,6},{6,10},{... | collective-permute-start | bytes 737288 | tf_op jit(solution)/shard_map/ppermute | solution.py:28
  12.0 8.1 %collective-permute-start.1 = (s32[6]{0:T(128)S(1)}, s32[6]{0:T(128)S(1)}, u32[]{:S(2)}, u32[]{:S(2)}) collective-permute-start(s32[6]{0:T(128)S(1)} %copy-done.8), channel_id=1, source_target_pairs={{0,4},{4,8},{8,12},{12,0},{1,5},{5,9},{9,13},{13,1},{2,6},{6,10},{... | collective-permute-start | bytes 80 | tf_op jit(solution)/shard_map/ppermute | solution.py:28
  20.1 23.5 %collective-permute-start.2 = (bf16[96,1280]{1,0:T(8,128)(2,1)}, bf16[96,1280]{1,0:T(8,128)(2,1)}, u32[]{:S(2)}, u32[]{:S(2)}) collective-permute-start(bf16[96,1280]{1,0:T(8,128)(2,1)} %collective-permute-done), channel_id=1, source_target_pairs={{0,4},{4,8},{8,12},{12,0},{1,5},{5,9},{9,13},{13,1},{2,6},{6,10},{... | collective-permute-start | bytes 737288 | tf_op jit(solution)/shard_map/ppermute | solution.py:28
  38.2 5.4 %collective-permute-start.3 = (s32[6]{0:T(128)S(1)}, s32[6]{0:T(128)S(1)}, u32[]{:S(2)}, u32[]{:S(2)}) collective-permute-start(s32[6]{0:T(128)S(1)} %collective-permute-done.1), channel_id=1, source_target_pairs={{0,4},{4,8},{8,12},{12,0},{1,5},{5,9},{9,13},{13,1},{2,6},{6,10},{... | collective-permute-start | bytes 80 | tf_op jit(solution)/shard_map/ppermute | solution.py:28
  43.6 33.8 %collective-permute-start.4 = (bf16[96,1280]{1,0:T(8,128)(2,1)}, bf16[96,1280]{1,0:T(8,128)(2,1)}, u32[]{:S(2)}, u32[]{:S(2)}) collective-permute-start(bf16[96,1280]{1,0:T(8,128)(2,1)} %collective-permute-done.2), channel_id=1, source_target_pairs={{0,4},{4,8},{8,12},{12,0},{1,5},{5,9},{9,13},{13,1},{2,6},{6,10},{... | collective-permute-start | bytes 737288 | tf_op jit(solution)/shard_map/ppermute | solution.py:28
  44.6 39.3 %collective-permute-start.13 = (bf16[4,96,640]{2,1,0:T(8,128)(2,1)}, bf16[4,96,640]{2,1,0:T(8,128)(2,1)}, u32[]{:S(2)}, u32[]{:S(2)}) collective-permute-start(bf16[4,96,640]{2,1,0:T(8,128)(2,1)} %bitcast.9.rest_0_), channel_id=1, source_target_pairs={{0,4},{4,8},{8,12},{12,0},{1,5},{5,9},{9,13},{13,1},{2,6},{6,10},{... | collective-permute-start | bytes 1474568 | tf_op jit(solution)/shard_map/ppermute | solution.py:28
  45.6 31.8 %collective-permute-start.5 = (s32[6]{0:T(128)S(1)}, s32[6]{0:T(128)S(1)}, u32[]{:S(2)}, u32[]{:S(2)}) collective-permute-start(s32[6]{0:T(128)S(1)} %collective-permute-done.3), channel_id=1, source_target_pairs={{0,4},{4,8},{8,12},{12,0},{1,5},{5,9},{9,13},{13,1},{2,6},{6,10},{... | collective-permute-start | bytes 80 | tf_op jit(solution)/shard_map/ppermute | solution.py:28
  81.0 9.5 %collective-permute-start.6 = (bf16[192,1280]{1,0:T(8,128)(2,1)}, bf16[192,1280]{1,0:T(8,128)(2,1)}, u32[]{:S(2)}, u32[]{:S(2)}) collective-permute-start(bf16[192,1280]{1,0:T(8,128)(2,1)} %dynamic-slice_convert_fusion), channel_id=1, source_target_pairs={{0,1},{1,0},{2,3},{3,2},{4,5},{5,4},{6,7},{7,6},{8,9},{9,8},{10,11... | collective-permute-start | bytes 1474568 | tf_op jit(solution)/shard_map/ppermute | solution.py:24
  83.3 12.4 %collective-permute-start.9 = (bf16[128,1280]{1,0:T(8,128)(2,1)}, bf16[128,1280]{1,0:T(8,128)(2,1)}, u32[]{:S(2)}, u32[]{:S(2)}) collective-permute-start(bf16[128,1280]{1,0:T(8,128)(2,1)} %dynamic-slice_convert_fusion.1), channel_id=1, source_target_pairs={{0,1},{1,0},{2,3},{3,2},{4,5},{5,4},{6,7},{7,6},{8,9},{9,8},{10,11... | collective-permute-start | bytes 983048 | tf_op jit(solution)/shard_map/ppermute | solution.py:24
  83.8 24.9 %collective-permute-start.14 = (bf16[4,96,640]{2,1,0:T(8,128)(2,1)}, bf16[4,96,640]{2,1,0:T(8,128)(2,1)}, u32[]{:S(2)}, u32[]{:S(2)}) collective-permute-start(bf16[4,96,640]{2,1,0:T(8,128)(2,1)} %collective-permute-done.13.rest_1_), channel_id=1, source_target_pairs={{0,4},{4,8},{8,12},{12,0},{1,5},{5,9},{9,13},{13,1},{2,6},{6,10},{... | collective-permute-start | bytes 1474568 | tf_op jit(solution)/shard_map/ppermute | solution.py:28
  92.8 16.6 %collective-permute-start.7 = (bf16[192,1280]{1,0:T(8,128)(2,1)}, bf16[192,1280]{1,0:T(8,128)(2,1)}, u32[]{:S(2)}, u32[]{:S(2)}) collective-permute-start(bf16[192,1280]{1,0:T(8,128)(2,1)} %fusion.8), channel_id=1, source_target_pairs={{0,2},{2,0},{1,3},{3,1},{4,6},{6,4},{5,7},{7,5},{8,10},{10,8},{9,1... | collective-permute-start | bytes 1474568 | tf_op jit(solution)/shard_map/ppermute | solution.py:24
  95.6 42.7 %collective-permute-start.12 = (bf16[4,256,640]{2,1,0:T(8,128)(2,1)}, bf16[4,256,640]{2,1,0:T(8,128)(2,1)}, u32[]{:S(2)}, u32[]{:S(2)}) collective-permute-start(bf16[4,256,640]{2,1,0:T(8,128)(2,1)} %bitcast.6.q_own), channel_id=1, source_target_pairs={{0,1},{1,0},{2,3},{3,2},{4,5},{5,4},{6,7},{7,6},{8,9},{9,8},{10,11... | collective-permute-start | bytes 3932168 | tf_op jit(solution)/shard_map/ppermute | solution.py:24
  97.0 15.9 %collective-permute-start.10 = (bf16[128,1280]{1,0:T(8,128)(2,1)S(1)}, bf16[128,1280]{1,0:T(8,128)(2,1)S(1)}, u32[]{:S(2)}, u32[]{:S(2)}) collective-permute-start(bf16[128,1280]{1,0:T(8,128)(2,1)S(1)} %fusion.9), channel_id=1, source_target_pairs={{0,2},{2,0},{1,3},{3,1},{4,6},{6,4},{5,7},{7,5},{8,10},{10,8},{9,1... | collective-permute-start | bytes 983048 | tf_op jit(solution)/shard_map/ppermute | solution.py:24
  108.7 21.9 %collective-permute-start.15 = (bf16[4,96,640]{2,1,0:T(8,128)(2,1)}, bf16[4,96,640]{2,1,0:T(8,128)(2,1)}, u32[]{:S(2)}, u32[]{:S(2)}) collective-permute-start(bf16[4,96,640]{2,1,0:T(8,128)(2,1)} %collective-permute-done.14.rest_2_), channel_id=1, source_target_pairs={{0,4},{4,8},{8,12},{12,0},{1,5},{5,9},{9,13},{13,1},{2,6},{6,10},{... | collective-permute-start | bytes 1474568 | tf_op jit(solution)/shard_map/ppermute | solution.py:28
  111.9 18.7 %collective-permute-start.8 = (bf16[192,1280]{1,0:T(8,128)(2,1)}, bf16[192,1280]{1,0:T(8,128)(2,1)}, u32[]{:S(2)}, u32[]{:S(2)}) collective-permute-start(bf16[192,1280]{1,0:T(8,128)(2,1)} %add_convert_fusion), channel_id=1, source_target_pairs={{0,1},{1,0},{2,3},{3,2},{4,5},{5,4},{6,7},{7,6},{8,9},{9,8},{10,11... | collective-permute-start | bytes 1474568 | tf_op jit(solution)/shard_map/ppermute | solution.py:24
  114.7 23.6 %collective-permute-start.16 = (bf16[4,96,640]{2,1,0:T(8,128)(2,1)}, bf16[4,96,640]{2,1,0:T(8,128)(2,1)}, u32[]{:S(2)}, u32[]{:S(2)}) collective-permute-start(bf16[4,96,640]{2,1,0:T(8,128)(2,1)} %bitcast.9.rest_0_), channel_id=1, source_target_pairs={{0,1},{1,0},{2,3},{3,2},{4,5},{5,4},{6,7},{7,6},{8,9},{9,8},{10,11... | collective-permute-start | bytes 1474568 | tf_op jit(solution)/shard_map/ppermute | solution.py:24
  116.7 21.6 %collective-permute-start.17 = (bf16[4,96,640]{2,1,0:T(8,128)(2,1)}, bf16[4,96,640]{2,1,0:T(8,128)(2,1)}, u32[]{:S(2)}, u32[]{:S(2)}) collective-permute-start(bf16[4,96,640]{2,1,0:T(8,128)(2,1)} %collective-permute-done.13.rest_1_), channel_id=1, source_target_pairs={{0,1},{1,0},{2,3},{3,2},{4,5},{5,4},{6,7},{7,6},{8,9},{9,8},{10,11... | collective-permute-start | bytes 1474568 | tf_op jit(solution)/shard_map/ppermute | solution.py:24
  130.7 7.7 %collective-permute-start.18 = (bf16[4,96,640]{2,1,0:T(8,128)(2,1)}, bf16[4,96,640]{2,1,0:T(8,128)(2,1)}, u32[]{:S(2)}, u32[]{:S(2)}) collective-permute-start(bf16[4,96,640]{2,1,0:T(8,128)(2,1)} %collective-permute-done.14.rest_2_), channel_id=1, source_target_pairs={{0,1},{1,0},{2,3},{3,2},{4,5},{5,4},{6,7},{7,6},{8,9},{9,8},{10,11... | collective-permute-start | bytes 1474568 | tf_op jit(solution)/shard_map/ppermute | solution.py:24
  130.7 7.7 %collective-permute-start.19 = (bf16[4,96,640]{2,1,0:T(8,128)(2,1)}, bf16[4,96,640]{2,1,0:T(8,128)(2,1)}, u32[]{:S(2)}, u32[]{:S(2)}) collective-permute-start(bf16[4,96,640]{2,1,0:T(8,128)(2,1)} %collective-permute-done.15.rest_3_), channel_id=1, source_target_pairs={{0,1},{1,0},{2,3},{3,2},{4,5},{5,4},{6,7},{7,6},{8,9},{9,8},{10,11... | collective-permute-start | bytes 1474568 | tf_op jit(solution)/shard_map/ppermute | solution.py:24
  234.8 5.5 %collective-permute-start.23 = (f32[16,6]{1,0:T(8,128)S(1)}, f32[16,6]{1,0:T(8,128)S(1)}, u32[]{:S(2)}, u32[]{:S(2)}) collective-permute-start(f32[16,6]{1,0:T(8,128)S(1)} %get-tuple-element.27), channel_id=1, source_target_pairs={{0,4},{4,8},{8,12},{12,0},{1,5},{5,9},{9,13},{13,1},{2,6},{6,10},{... | collective-permute-start | bytes 1160 | tf_op jit(solution)/shard_map/ppermute | solution.py:289
  234.8 5.4 %collective-permute-start.24 = (f32[16,6]{1,0:T(8,128)S(1)}, f32[16,6]{1,0:T(8,128)S(1)}, u32[]{:S(2)}, u32[]{:S(2)}) collective-permute-start(f32[16,6]{1,0:T(8,128)S(1)} %get-tuple-element.29), channel_id=1, source_target_pairs={{0,8},{4,12},{8,0},{12,4},{1,9},{5,13},{9,1},{13,5},{2,10},{6,14},... | collective-permute-start | bytes 1160 | tf_op jit(solution)/shard_map/ppermute | solution.py:289
  236.9 3.9 %collective-permute-start.25 = (f32[16,6]{1,0:T(8,128)S(1)}, f32[16,6]{1,0:T(8,128)S(1)}, u32[]{:S(2)}, u32[]{:S(2)}) collective-permute-start(f32[16,6]{1,0:T(8,128)S(1)} %get-tuple-element.28), channel_id=1, source_target_pairs={{0,12},{4,0},{8,4},{12,8},{1,13},{5,1},{9,5},{13,9},{2,14},{6,2},{... | collective-permute-start | bytes 1160 | tf_op jit(solution)/shard_map/ppermute | solution.py:289
  (15 other events, 238.1 us)
Sparse Core Ops, SparseCore 0:
  9.6 79.7 all-gather.4
  91.5 71.0 all-gather.2

commit v4 on v3

--- a/solution.py
+++ b/solution.py
@@ -236,10 +236,8 @@
         mine = lax.dynamic_slice_in_dim(hidden_basis, grp * (rows // 2), rows // 2, 1)
     mine = [mine[b : b + chunk] for b in range(0, blocks, chunk)]
     acts, *mine = lax.optimization_barrier((ex_acts.reshape(e_rows, input_cols), *mine))
-    full = [
-        lax.all_gather(part, ("dp", "groups") if share else "dp", axis=1, tiled=True)
-        for part in mine
-    ]
+    both = ("dp", "groups") if share else "dp"
+    full = [lax.all_gather(mine[0], both, axis=1, tiled=True)]
 
     w = weights(eigenvalues)
     acts, ids = [acts], [ex_ids]
@@ -257,6 +255,9 @@
     e_raw = jnp.transpose(ex_grads.reshape(e_rows, blocks, width) * keep, (1, 0, 2))
     q_raw = jnp.transpose(query_grads.reshape(q_rows, blocks, width), (1, 0, 2))
     xs = ring(e_raw, n)
+    if len(mine) > 1:
+        xs[-1], *later = lax.optimization_barrier((xs[-1], *mine[1:]))
+        full += [lax.all_gather(part, both, axis=1, tiled=True) for part in later]
     zs = [swap(x, "sub") for x in xs]
     q_oth = swap(q_raw, "sub")
 

time: 249 us -> 252 us (1.012)
  waiting for transfers between devices: 72.6 us -> 83 us
  starting transfers between devices: 26.1 us -> 17.1 us
    ppermute x11, waiting for transfers between devices: 2.38 us -> 12.2 us  [swap(): return lax.ppermute(x, axis, [(0, 1), (1, 0)])]
    ppermute x9, starting transfers between devices: 16.6 us -> 8.23 us  [step_along(): return lax.ppermute(x, 'dp', [(i, (i + 1) % n) for i in range(n)])]
  transfers between devices with their start and end apart: 28 -> 28, of which waited for: 11 -> 12; matrix products, arithmetic and copies ran while one was open for 10% -> 10% of each run, Pallas kernels for 25% -> 24%
where the time goes in v4:
time: 252 us; the launch traced here: 251 us
  Pallas kernels  107 us (42%)
  waiting for transfers between devices  83 us (33%)
  starting transfers between devices  17.1 us (7%)
  other arithmetic  16.1 us (6%)
  between operations  13.6 us (5%)
  local copies, waits for them, and re-layouts  10.8 us (4%)
  matrix products  3.83 us (2%)
    pallas_call x2, Pallas kernels, chunk_scores(): pl.pallas_call(functools.partial(score_kernel, n, q_count, seq, first), o...  90.5 us
    ppermute x9, waiting for transfers between devices, step_along(): return lax.ppermute(x, 'dp', [(i, (i + 1) % n) for i in range(n)])  66.5 us
    pallas_call x1, Pallas kernels, weights(): pl.pallas_call(functools.partial(weight_kernel, blocks, step), grid=(bloc...  16.1 us
    ppermute x11, waiting for transfers between devices, swap(): return lax.ppermute(x, axis, [(0, 1), (1, 0)])  12.2 us
    ppermute x9, starting transfers between devices, step_along(): return lax.ppermute(x, 'dp', [(i, (i + 1) % n) for i in range(n)])  8.23 us
  transfers between devices with their start and end apart: 28, of which 12 were waited for; matrix products, arithmetic and copies ran while one was open for 10% of the time, Pallas kernels for 24%

profile of v4, /device:TPU:0, one launch (start us, length us, event | category | flops | bytes accessed | tf_op | source)
XLA Modules:
  0.0 251.1 jit_solution(12830799958096984147)
XLA Ops:
  6.6 2.2 constant_dynamic-slice_fusion.4
  8.9 3.1 %collective-permute-start = (bf16[96,1280]{1,0:T(8,128)(2,1)S(1)}, bf16[96,1280]{1,0:T(8,128)(2,1)}, u32[]{:S(2)}, u32[]{:S(2)}) collective-permute-start(bf16[96,1280]{1,0:T(8,128)(2,1)S(1)} %bitcast.19), channel_id=1, source_target_pairs={{0,4},{4,8},{8,12},{12,0},{1,5},{5,9},{9,13},{13,1},{2,6},{6,10},{... | collective-permute-start | bytes 737288 | tf_op jit(solution)/shard_map/ppermute | solution.py:28
  13.6 1.9 copy.15
  15.5 1.9 bitcast_multiply_fusion
  17.5 2.6 %collective-permute-done.1 = s32[6]{0:T(128)S(1)} collective-permute-done((s32[6]{0:T(128)S(1)}, s32[6]{0:T(128)S(1)}, u32[]{:S(2)}, u32[]{:S(2)}) %collective-permute-start.1) | collective-permute-done | bytes 56 | tf_op jit(solution)/shard_map/ppermute | solution.py:28
  21.4 16.1 %weights.1.w = f32[5120,640]{1,0:T(8,128)} custom-call(f32[1280,4,640]{2,1,0:T(4,128)} %lam.1), custom_call_target="tpu_custom_call" | custom-call | flops 13107200 | bytes 26214400 | tf_op jit(solution)/shard_map/weights/pallas_call | solution.py:71
  37.5 1.6 collective-permute-start.3
  39.2 14.0 %collective-permute-done.3 = s32[6]{0:T(128)S(1)} collective-permute-done((s32[6]{0:T(128)S(1)}, s32[6]{0:T(128)S(1)}, u32[]{:S(2)}, u32[]{:S(2)}) %collective-permute-start.3) | collective-permute-done | bytes 56 | tf_op jit(solution)/shard_map/ppermute | solution.py:28
  53.8 15.1 %collective-permute-done.5 = s32[6]{0:T(128)S(1)} collective-permute-done((s32[6]{0:T(128)S(1)}, s32[6]{0:T(128)S(1)}, u32[]{:S(2)}, u32[]{:S(2)}) %collective-permute-start.5) | collective-permute-done | bytes 56 | tf_op jit(solution)/shard_map/ppermute | solution.py:28
  68.9 2.6 %fusion = f32[384,1280]{1,0:T(8,128)S(1)} fusion(bf16[1280,1280]{1,0:T(8,128)(2,1)S(1)} %copy-done, bf16[96,1280]{1,0:T(8,128)(2,1)} %collective-permute-done.4, bf16[96,1280]{1,0:T(8,128)(2,1)} %collective-permute-done.2, bf16[96,1280]{1,0:T(8,128)(2,1)} %collective-permute-done, bf16[96,1280]{1,0:T(8,128)(2,1)S(1)} %bitcast.20), kind=kOutput, calls=%fused_computation | convolution fusion | flops 1262223360 | bytes 6225920 | tf_op jit(solution)/shard_map/dot_general | solution.py:20
  72.6 15.4 %collective-permute-done.14.rest_2_ = bf16[4,96,640]{2,1,0:T(8,128)(2,1)} collective-permute-done((bf16[4,96,640]{2,1,0:T(8,128)(2,1)}, bf16[4,96,640]{2,1,0:T(8,128)(2,1)}, u32[]{:S(2)}, u32[]{:S(2)}) %collective-permute-start.14) | collective-permute-done | bytes 491552 | tf_op jit(solution)/shard_map/ppermute | solution.py:28
  90.3 19.3 %collective-permute-done.15.rest_3_ = bf16[4,96,640]{2,1,0:T(8,128)(2,1)} collective-permute-done((bf16[4,96,640]{2,1,0:T(8,128)(2,1)}, bf16[4,96,640]{2,1,0:T(8,128)(2,1)}, u32[]{:S(2)}, u32[]{:S(2)}) %collective-permute-start.15) | collective-permute-done | bytes 491552 | tf_op jit(solution)/shard_map/ppermute | solution.py:28
  109.6 2.3 fusion.8
  116.7 9.7 %collective-permute-done.7 = bf16[192,1280]{1,0:T(8,128)(2,1)} collective-permute-done((bf16[192,1280]{1,0:T(8,128)(2,1)}, bf16[192,1280]{1,0:T(8,128)(2,1)}, u32[]{:S(2)}, u32[]{:S(2)}) %collective-permute-start.7) | collective-permute-done | bytes 491552 | tf_op jit(solution)/shard_map/ppermute | solution.py:24
  126.4 2.5 add_convert_fusion
  130.0 1.8 add_convert_fusion.1
  134.3 2.3 maximum_select_fusion.1
  136.6 2.3 copy.13
  138.9 2.7 %maximum_select_fusion.ei = bf16[384,1280]{1,0:T(8,128)(2,1)} fusion(bf16[192,1280]{1,0:T(8,128)(2,1)} %collective-permute-done.8, bf16[192,1280]{1,0:T(8,128)(2,1)} %add_convert_fusion, pred[]{:T(512)S(6)} %eq.8), kind=kLoop, calls=%fused_computation.8 | loop fusion | flops 4423680 | bytes 1966081 | tf_op jit(solution)/shard_map/jit(_where)/select_n | solution.py:206
  141.7 45.2 %chunk_scores.2 = f32[16,24,128]{2,1,0:T(8,128)} custom-call(s32[1]{0:T(128)} %bitcast.idx, bf16[384,1280]{1,0:T(8,128)(2,1)} %maximum_select_fusion.ei, bf16[2,1280,128]{2,1,0:T(8,128)(2,1)} %bitcast.16, f32[5120,640]{1,0:T(8,128)} %weights.1.w, bf16[2,1280,640]{2,1,0:T(8,128)(2,1)} %all-gather.3.cloned.1.call-done.basis, ...), custom_call_target="tpu_custom_call" | custom-call | flops 33554432000 | bytes 12582912 | tf_op jit(solution)/shard_map/chunk_scores/pallas_call | solution.py:172
  186.9 45.3 %chunk_scores.3 = f32[16,24,128]{2,1,0:T(8,128)} custom-call(s32[1]{0:T(128)} %bitcast.idx, bf16[384,1280]{1,0:T(8,128)(2,1)} %maximum_select_fusion.ei, bf16[2,1280,128]{2,1,0:T(8,128)(2,1)} %bitcast.17, f32[5120,640]{1,0:T(8,128)} %weights.1.w, bf16[2,1280,640]{2,1,0:T(8,128)(2,1)} %all-gather.5.cloned.1.call-done.basis, ...), custom_call_target="tpu_custom_call" | custom-call | flops 33554432000 | bytes 12582912 | tf_op jit(solution)/shard_map/chunk_scores/pallas_call | solution.py:172
  235.3 1.8 collective-permute-done.21
  237.9 3.4 %collective-permute-start.25 = (f32[16,6]{1,0:T(8,128)S(1)}, f32[16,6]{1,0:T(8,128)S(1)}, u32[]{:S(2)}, u32[]{:S(2)}) collective-permute-start(f32[16,6]{1,0:T(8,128)S(1)} %get-tuple-element.32), channel_id=1, source_target_pairs={{0,12},{4,0},{8,4},{12,8},{1,13},{5,1},{9,5},{13,9},{2,14},{6,2},{... | collective-permute-start | bytes 1160 | tf_op jit(solution)/shard_map/ppermute | solution.py:290
  241.3 1.6 collective-permute-done.23
  (81 shorter events, 20.6 us)
Async XLA Ops:
  6.5 135.1 %all-gather.3.cloned.1.call-start = ((), (), s32[]{:S(2)}) async-start(), calls=%async_computation | async-start | bytes 3686400 | tf_op jit(solution)/shard_map/all_gather | solution.py:240
  8.9 178.1 %all-gather.5.cloned.1.call-start = ((), (), s32[]{:S(2)}) async-start(), calls=%async_computation.1 | async-start | bytes 3686400 | tf_op jit(solution)/shard_map/all_gather | solution.py:260
  8.9 11.2 %collective-permute-start = (bf16[96,1280]{1,0:T(8,128)(2,1)S(1)}, bf16[96,1280]{1,0:T(8,128)(2,1)}, u32[]{:S(2)}, u32[]{:S(2)}) collective-permute-start(bf16[96,1280]{1,0:T(8,128)(2,1)S(1)} %bitcast.19), channel_id=1, source_target_pairs={{0,4},{4,8},{8,12},{12,0},{1,5},{5,9},{9,13},{13,1},{2,6},{6,10},{... | collective-permute-start | bytes 737288 | tf_op jit(solution)/shard_map/ppermute | solution.py:28
  12.0 8.1 %collective-permute-start.1 = (s32[6]{0:T(128)S(1)}, s32[6]{0:T(128)S(1)}, u32[]{:S(2)}, u32[]{:S(2)}) collective-permute-start(s32[6]{0:T(128)S(1)} %copy-done.7), channel_id=1, source_target_pairs={{0,4},{4,8},{8,12},{12,0},{1,5},{5,9},{9,13},{13,1},{2,6},{6,10},{... | collective-permute-start | bytes 80 | tf_op jit(solution)/shard_map/ppermute | solution.py:28
  20.1 33.0 %collective-permute-start.2 = (bf16[96,1280]{1,0:T(8,128)(2,1)}, bf16[96,1280]{1,0:T(8,128)(2,1)}, u32[]{:S(2)}, u32[]{:S(2)}) collective-permute-start(bf16[96,1280]{1,0:T(8,128)(2,1)} %collective-permute-done), channel_id=1, source_target_pairs={{0,4},{4,8},{8,12},{12,0},{1,5},{5,9},{9,13},{13,1},{2,6},{6,10},{... | collective-permute-start | bytes 737288 | tf_op jit(solution)/shard_map/ppermute | solution.py:28
  20.1 33.1 %collective-permute-start.13 = (bf16[4,96,640]{2,1,0:T(8,128)(2,1)}, bf16[4,96,640]{2,1,0:T(8,128)(2,1)}, u32[]{:S(2)}, u32[]{:S(2)}) collective-permute-start(bf16[4,96,640]{2,1,0:T(8,128)(2,1)} %bitcast.9.rest_0_), channel_id=1, source_target_pairs={{0,4},{4,8},{8,12},{12,0},{1,5},{5,9},{9,13},{13,1},{2,6},{6,10},{... | collective-permute-start | bytes 1474568 | tf_op jit(solution)/shard_map/ppermute | solution.py:28
  37.5 15.6 %collective-permute-start.3 = (s32[6]{0:T(128)S(1)}, s32[6]{0:T(128)S(1)}, u32[]{:S(2)}, u32[]{:S(2)}) collective-permute-start(s32[6]{0:T(128)S(1)} %collective-permute-done.1), channel_id=1, source_target_pairs={{0,4},{4,8},{8,12},{12,0},{1,5},{5,9},{9,13},{13,1},{2,6},{6,10},{... | collective-permute-start | bytes 80 | tf_op jit(solution)/shard_map/ppermute | solution.py:28
  53.1 15.8 %collective-permute-start.4 = (bf16[96,1280]{1,0:T(8,128)(2,1)}, bf16[96,1280]{1,0:T(8,128)(2,1)}, u32[]{:S(2)}, u32[]{:S(2)}) collective-permute-start(bf16[96,1280]{1,0:T(8,128)(2,1)} %collective-permute-done.2), channel_id=1, source_target_pairs={{0,4},{4,8},{8,12},{12,0},{1,5},{5,9},{9,13},{13,1},{2,6},{6,10},{... | collective-permute-start | bytes 737288 | tf_op jit(solution)/shard_map/ppermute | solution.py:28
  53.1 15.8 %collective-permute-start.5 = (s32[6]{0:T(128)S(1)}, s32[6]{0:T(128)S(1)}, u32[]{:S(2)}, u32[]{:S(2)}) collective-permute-start(s32[6]{0:T(128)S(1)} %collective-permute-done.3), channel_id=1, source_target_pairs={{0,4},{4,8},{8,12},{12,0},{1,5},{5,9},{9,13},{13,1},{2,6},{6,10},{... | collective-permute-start | bytes 80 | tf_op jit(solution)/shard_map/ppermute | solution.py:28
  53.2 34.8 %collective-permute-start.14 = (bf16[4,96,640]{2,1,0:T(8,128)(2,1)}, bf16[4,96,640]{2,1,0:T(8,128)(2,1)}, u32[]{:S(2)}, u32[]{:S(2)}) collective-permute-start(bf16[4,96,640]{2,1,0:T(8,128)(2,1)} %collective-permute-done.13.rest_1_), channel_id=1, source_target_pairs={{0,4},{4,8},{8,12},{12,0},{1,5},{5,9},{9,13},{13,1},{2,6},{6,10},{... | collective-permute-start | bytes 1474568 | tf_op jit(solution)/shard_map/ppermute | solution.py:28
  72.6 37.0 %collective-permute-start.6 = (bf16[192,1280]{1,0:T(8,128)(2,1)}, bf16[192,1280]{1,0:T(8,128)(2,1)}, u32[]{:S(2)}, u32[]{:S(2)}) collective-permute-start(bf16[192,1280]{1,0:T(8,128)(2,1)} %dynamic-slice_convert_fusion), channel_id=1, source_target_pairs={{0,1},{1,0},{2,3},{3,2},{4,5},{5,4},{6,7},{7,6},{8,9},{9,8},{10,11... | collective-permute-start | bytes 1474568 | tf_op jit(solution)/shard_map/ppermute | solution.py:24
  88.0 21.6 %collective-permute-start.15 = (bf16[4,96,640]{2,1,0:T(8,128)(2,1)}, bf16[4,96,640]{2,1,0:T(8,128)(2,1)}, u32[]{:S(2)}, u32[]{:S(2)}) collective-permute-start(bf16[4,96,640]{2,1,0:T(8,128)(2,1)} %collective-permute-done.14.rest_2_), channel_id=1, source_target_pairs={{0,4},{4,8},{8,12},{12,0},{1,5},{5,9},{9,13},{13,1},{2,6},{6,10},{... | collective-permute-start | bytes 1474568 | tf_op jit(solution)/shard_map/ppermute | solution.py:28
  90.3 23.8 %collective-permute-start.9 = (bf16[128,1280]{1,0:T(8,128)(2,1)}, bf16[128,1280]{1,0:T(8,128)(2,1)}, u32[]{:S(2)}, u32[]{:S(2)}) collective-permute-start(bf16[128,1280]{1,0:T(8,128)(2,1)} %dynamic-slice_convert_fusion.1), channel_id=1, source_target_pairs={{0,1},{1,0},{2,3},{3,2},{4,5},{5,4},{6,7},{7,6},{8,9},{9,8},{10,11... | collective-permute-start | bytes 983048 | tf_op jit(solution)/shard_map/ppermute | solution.py:24
  111.9 14.5 %collective-permute-start.7 = (bf16[192,1280]{1,0:T(8,128)(2,1)}, bf16[192,1280]{1,0:T(8,128)(2,1)}, u32[]{:S(2)}, u32[]{:S(2)}) collective-permute-start(bf16[192,1280]{1,0:T(8,128)(2,1)} %fusion.8), channel_id=1, source_target_pairs={{0,2},{2,0},{1,3},{3,1},{4,6},{6,4},{5,7},{7,5},{8,10},{10,8},{9,1... | collective-permute-start | bytes 1474568 | tf_op jit(solution)/shard_map/ppermute | solution.py:24
  114.0 27.6 %collective-permute-start.12 = (bf16[4,256,640]{2,1,0:T(8,128)(2,1)}, bf16[4,256,640]{2,1,0:T(8,128)(2,1)}, u32[]{:S(2)}, u32[]{:S(2)}) collective-permute-start(bf16[4,256,640]{2,1,0:T(8,128)(2,1)} %bitcast.6.q_own), channel_id=1, source_target_pairs={{0,1},{1,0},{2,3},{3,2},{4,5},{5,4},{6,7},{7,6},{8,9},{9,8},{10,11... | collective-permute-start | bytes 3932168 | tf_op jit(solution)/shard_map/ppermute | solution.py:24
  115.5 14.5 %collective-permute-start.10 = (bf16[128,1280]{1,0:T(8,128)(2,1)S(1)}, bf16[128,1280]{1,0:T(8,128)(2,1)S(1)}, u32[]{:S(2)}, u32[]{:S(2)}) collective-permute-start(bf16[128,1280]{1,0:T(8,128)(2,1)S(1)} %fusion.9), channel_id=1, source_target_pairs={{0,2},{2,0},{1,3},{3,1},{4,6},{6,4},{5,7},{7,5},{8,10},{10,8},{9,1... | collective-permute-start | bytes 983048 | tf_op jit(solution)/shard_map/ppermute | solution.py:24
  128.9 5.1 %collective-permute-start.8 = (bf16[192,1280]{1,0:T(8,128)(2,1)}, bf16[192,1280]{1,0:T(8,128)(2,1)}, u32[]{:S(2)}, u32[]{:S(2)}) collective-permute-start(bf16[192,1280]{1,0:T(8,128)(2,1)} %add_convert_fusion), channel_id=1, source_target_pairs={{0,1},{1,0},{2,3},{3,2},{4,5},{5,4},{6,7},{7,6},{8,9},{9,8},{10,11... | collective-permute-start | bytes 1474568 | tf_op jit(solution)/shard_map/ppermute | solution.py:24
  131.8 9.8 %collective-permute-start.16 = (bf16[4,96,640]{2,1,0:T(8,128)(2,1)}, bf16[4,96,640]{2,1,0:T(8,128)(2,1)}, u32[]{:S(2)}, u32[]{:S(2)}) collective-permute-start(bf16[4,96,640]{2,1,0:T(8,128)(2,1)} %bitcast.9.rest_0_), channel_id=1, source_target_pairs={{0,1},{1,0},{2,3},{3,2},{4,5},{5,4},{6,7},{7,6},{8,9},{9,8},{10,11... | collective-permute-start | bytes 1474568 | tf_op jit(solution)/shard_map/ppermute | solution.py:24
  132.3 9.3 %collective-permute-start.17 = (bf16[4,96,640]{2,1,0:T(8,128)(2,1)}, bf16[4,96,640]{2,1,0:T(8,128)(2,1)}, u32[]{:S(2)}, u32[]{:S(2)}) collective-permute-start(bf16[4,96,640]{2,1,0:T(8,128)(2,1)} %collective-permute-done.13.rest_1_), channel_id=1, source_target_pairs={{0,1},{1,0},{2,3},{3,2},{4,5},{5,4},{6,7},{7,6},{8,9},{9,8},{10,11... | collective-permute-start | bytes 1474568 | tf_op jit(solution)/shard_map/ppermute | solution.py:24
  133.8 7.9 %collective-permute-start.18 = (bf16[4,96,640]{2,1,0:T(8,128)(2,1)}, bf16[4,96,640]{2,1,0:T(8,128)(2,1)}, u32[]{:S(2)}, u32[]{:S(2)}) collective-permute-start(bf16[4,96,640]{2,1,0:T(8,128)(2,1)} %collective-permute-done.14.rest_2_), channel_id=1, source_target_pairs={{0,1},{1,0},{2,3},{3,2},{4,5},{5,4},{6,7},{7,6},{8,9},{9,8},{10,11... | collective-permute-start | bytes 1474568 | tf_op jit(solution)/shard_map/ppermute | solution.py:24
  133.9 7.7 %collective-permute-start.19 = (bf16[4,96,640]{2,1,0:T(8,128)(2,1)}, bf16[4,96,640]{2,1,0:T(8,128)(2,1)}, u32[]{:S(2)}, u32[]{:S(2)}) collective-permute-start(bf16[4,96,640]{2,1,0:T(8,128)(2,1)} %collective-permute-done.15.rest_3_), channel_id=1, source_target_pairs={{0,1},{1,0},{2,3},{3,2},{4,5},{5,4},{6,7},{7,6},{8,9},{9,8},{10,11... | collective-permute-start | bytes 1474568 | tf_op jit(solution)/shard_map/ppermute | solution.py:24
  237.5 5.5 %collective-permute-start.23 = (f32[16,6]{1,0:T(8,128)S(1)}, f32[16,6]{1,0:T(8,128)S(1)}, u32[]{:S(2)}, u32[]{:S(2)}) collective-permute-start(f32[16,6]{1,0:T(8,128)S(1)} %get-tuple-element.31), channel_id=1, source_target_pairs={{0,4},{4,8},{8,12},{12,0},{1,5},{5,9},{9,13},{13,1},{2,6},{6,10},{... | collective-permute-start | bytes 1160 | tf_op jit(solution)/shard_map/ppermute | solution.py:290
  237.5 5.4 %collective-permute-start.24 = (f32[16,6]{1,0:T(8,128)S(1)}, f32[16,6]{1,0:T(8,128)S(1)}, u32[]{:S(2)}, u32[]{:S(2)}) collective-permute-start(f32[16,6]{1,0:T(8,128)S(1)} %get-tuple-element.33), channel_id=1, source_target_pairs={{0,8},{4,12},{8,0},{12,4},{1,9},{5,13},{9,1},{13,5},{2,10},{6,14},... | collective-permute-start | bytes 1160 | tf_op jit(solution)/shard_map/ppermute | solution.py:290
  237.9 5.6 %collective-permute-start.25 = (f32[16,6]{1,0:T(8,128)S(1)}, f32[16,6]{1,0:T(8,128)S(1)}, u32[]{:S(2)}, u32[]{:S(2)}) collective-permute-start(f32[16,6]{1,0:T(8,128)S(1)} %get-tuple-element.32), channel_id=1, source_target_pairs={{0,12},{4,0},{8,4},{12,8},{1,13},{5,1},{9,5},{13,9},{2,14},{6,2},{... | collective-permute-start | bytes 1160 | tf_op jit(solution)/shard_map/ppermute | solution.py:290
  (14 other events, 207.7 us)
Sparse Core Ops, SparseCore 0:
  9.6 96.4 all-gather.2
  109.7 59.6 all-gather.4
